TPU v7x, 512 devices: a whole 4x8x8 slice. The times are simulated.
512 devices in a mesh: dp: 32 (over y, z_hi), tensor: 16 (over x, z_lo, core).
Axes of the slice: x: 4, y: 8, z: 8 (z_hi: 4, z_lo: 2; z = z_hi * 2 + z_lo), core: 2. Of those that a mesh axis runs over, the one named last changes fastest.
Arguments:
- hidden: bfloat16 [1024, 5120], P('dp'), may hold values from -6 to 6
- query_base_matrix: bfloat16 [5120, 4096], P(None, 'tensor'), may hold values from -0.078125 to 0.078125
- input_side_factor: bfloat16 [5120, 64], P('dp'), may hold values from -0.078125 to 0.078125
- output_side_factor: bfloat16 [64, 16, 256], P(None, None, 'dp'), may hold values from -0.75 to 0.75
- query_norm_gain: float32 [128], replicated, may hold values from 0.5 to 2
- cached_key_heads: bfloat16 [1024, 16, 64, 128], P('dp', 'tensor'), may hold values from -240 to 240
- cached_value_heads: bfloat16 [1024, 16, 64, 128], P('dp', 'tensor'), may hold values from -6 to 6
- lengths: int32 [1024], P('dp'), may hold values from 1 to 64, as said below
Outputs:
- attended: bfloat16 [1024, 4096], P('dp', 'tensor')
Inputs may be any that keep to these rules, and one draw needn't show every extreme that they name: `lengths`: some row holds exactly 64 and some row exactly 1.
All inputs are finite; a program needn't handle non-finite values.
Results may differ from a plain program's by a relative error of at most 0.012.
The roundings to bfloat16 on the way count: a program that leaves them out, or rounds other values in their place, can miss the bound.
Values may be sent and summed in bfloat16 or wider, within the bound.
A program may use at most 64 MiB of HBM per device.

v0:
```python
import math

import jax
import jax.numpy as jnp
from jax import lax
from jax.sharding import PartitionSpec as P


def local(
    hidden,
    query_base_matrix,
    input_side_factor,
    output_side_factor,
    query_norm_gain,
    cached_key_heads,
    cached_value_heads,
    lengths,
):
    tensor_shard_index = lax.axis_index("tensor")
    columns = query_base_matrix.shape[1]
    head_dim = cached_key_heads.shape[3]
    local_column_slice = lax.dynamic_index_in_dim(
        output_side_factor, tensor_shard_index, 1, keepdims=False
    )
    up_block = lax.all_gather(local_column_slice, "dp", axis=1, tiled=True)
    adapter_update = jnp.dot(
        lax.all_gather(input_side_factor, "dp", axis=0, tiled=True),
        up_block,
        preferred_element_type=jnp.float32,
    )
    merged = (query_base_matrix.astype(jnp.float32) + adapter_update).astype(jnp.bfloat16)
    row_count = hidden.shape[0]
    query = jnp.dot(hidden, merged, preferred_element_type=jnp.float32)
    query = query.reshape(row_count, columns // head_dim, head_dim)
    inverse = lax.rsqrt(jnp.mean(query * query, axis=-1, keepdims=True) + 1e-06)
    normed = (query * inverse * query_norm_gain).astype(jnp.bfloat16)
    keys_local = cached_key_heads[:, 0]
    values_local = cached_value_heads[:, 0]
    scores = jnp.einsum(
        "rgd,rpd->rgp", normed, keys_local, preferred_element_type=jnp.float32
    ) / math.sqrt(head_dim)
    positions = lax.broadcasted_iota(jnp.int32, (1, 1, keys_local.shape[1]), 2)
    valid = positions < lengths[:, None, None]
    scores = jnp.where(valid, scores, -jnp.inf)
    highest = jnp.max(scores, axis=-1, keepdims=True)
    expo = jnp.exp(scores - highest)
    weights = (expo / jnp.sum(expo, axis=-1, keepdims=True)).astype(jnp.bfloat16)
    result = jnp.einsum("rgp,rpd->rgd", weights, values_local, preferred_element_type=jnp.float32)
    return result.reshape(row_count, columns).astype(jnp.bfloat16)


def solution(mesh):
    in_specs = (
        P("dp", None),
        P(None, "tensor"),
        P("dp", None),
        P(None, None, "dp"),
        P(),
        P("dp", "tensor", None, None),
        P("dp", "tensor", None, None),
        P("dp"),
    )
    out_specs = P("dp", "tensor")
    return jax.shard_map(local, mesh=mesh, in_specs=in_specs, out_specs=out_specs, check_vma=False)
```

profile of v0, /device:TPU:6, one launch (start us, length us, event | category | flops | bytes accessed | tf_op | source)
XLA Modules:
  0.0 184.5 jit_solution(2086908067020433535)
XLA Ops:
  0.0 0.0 copy-start
  0.0 0.7 constant_dynamic-slice_fusion
  0.7 87.5 %all-gather = bf16[64,1,256]{0,2,1:T(8,128)(2,1)S(1)} all-gather(bf16[64,1,8]{0,2,1:T(8,128)(2,1)S(1)} %constant_dynamic-slice_fusion), channel_id=2, replica_groups=mesh['dp'=32,'tensor'=16] {'dp'}, dimensions={2}, use_global_device_ids=true | all-gather | bytes 33792 | tf_op jit(solution)/shard_map/all_gather | solution.py:25
  88.2 84.2 %all-gather.1 = bf16[32,160,64]{1,2,0:T(8,128)(2,1)S(1)} all-gather(bf16[1,160,64]{1,2,0:T(8,128)(2,1)} %bitcast.33), channel_id=1, replica_groups=mesh['dp'=32,'tensor'=16] {'dp'}, dimensions={0}, use_global_device_ids=true | all-gather | bytes 675840 | tf_op jit(solution)/shard_map/all_gather | solution.py:27
  172.5 0.6 copy.11
  173.0 2.5 %reshape.40 = bf16[5120,64]{0,1:T(8,128)(2,1)} reshape(bf16[32,160,64]{1,0,2:T(8,128)(2,1)S(1)} %copy.11) | data formatting | bytes 1310720
  175.6 3.0 %copy.10 = bf16[5120,256]{0,1:T(8,128)(2,1)S(1)} copy(bf16[5120,256]{1,0:T(8,128)(2,1)} %param.9) | data formatting | bytes 5242880 | tf_op args[1]
  178.6 0.0 copy-start.1
  178.6 0.0 copy-start.2
  178.6 2.7 %fusion.6 = f32[32,256]{1,0:T(8,128)S(1)} fusion(bf16[32,5120]{1,0:T(8,128)(2,1)} %param.8, bf16[5120,64]{0,1:T(8,128)(2,1)} %reshape.40, bf16[5120,256]{0,1:T(8,128)(2,1)S(1)} %copy.10, bf16[64,1,256]{0,2,1:T(8,128)(2,1)S(1)} %all-gather), kind=kOutput, calls=%fused_computation.7 | convolution fusion | flops 255590400 | bytes 3670016 | tf_op jit(solution)/shard_map/dot_general | solution.py:33
  181.3 0.1 reshape.37
  181.4 0.1 multiply_reduce_fusion
  181.5 0.0 copy-done.1
  181.5 0.1 iota_compare_fusion
  181.6 0.0 copy-done.2
  181.6 1.5 fusion.7
  183.1 0.2 fusion.15
  183.3 0.0 copy-done
  183.3 0.5 convolution_convert_fusion
  183.8 0.6 copy.14
  (1 shorter events, 0.0 us)
Async XLA Ops:
  0.0 183.3 %copy-start = (bf16[32,1,64,128]{3,2,1,0:T(8,128)(2,1)S(1)}, bf16[32,1,64,128]{3,2,1,0:T(8,128)(2,1)}, u32[]{:S(2)}) copy-start(bf16[32,1,64,128]{3,2,1,0:T(8,128)(2,1)} %param.14) | copy-start | bytes 1572868
  178.6 3.0 %copy-start.1 = (s32[32]{0:T(128)S(1)}, s32[32]{0:T(128)}, u32[]{:S(2)}) copy-start(s32[32]{0:T(128)} %param.15) | copy-start | bytes 388
  178.6 3.1 %copy-start.2 = (f32[128]{0:T(128)S(1)}, f32[128]{0:T(128)}, u32[]{:S(2)}) copy-start(f32[128]{0:T(128)} %param.12) | copy-start | bytes 1540
where the time goes:
time: 185 us; the launch traced here: 184 us
  blocking collectives  172 us (93%)
  local copies, waits for them, and re-layouts  7.53 us (4%)
  matrix products  4.74 us (3%)
    all_gather x1, blocking collectives, local(): up_block = lax.all_gather(local_column_slice, 'dp', axis=1, tiled=True)  87.5 us
    all_gather x1, blocking collectives, local(): lax.all_gather(input_side_factor, 'dp', axis=0, tiled=True)  84.2 us
    unnamed x9, local copies, waits for them, and re-layouts  6.14 us

commit v1 on v0

v1 whole, which is shorter than its diff:
```python
import functools
import math

import jax
import jax.numpy as jnp
from jax import lax
from jax.experimental import pallas as pl
from jax.experimental.pallas import tpu as pltpu
from jax.sharding import PartitionSpec as P

MESH = pl.DeviceIdType.MESH
N_DP = 32
PACKED = 80
SLOT = PACKED + 32


def flip(bit, other):
    return lax.rem(bit + other, 2)


def bits_of(dp):
    y, zh = dp // 4, lax.rem(dp, 4)
    return y // 4, lax.rem(y // 2, 2), lax.rem(y, 2), zh // 2, lax.rem(zh, 2)


def index_of(y2, y1, y0, z1, z0):
    return y2 * 16 + y1 * 8 + y0 * 4 + z1 * 2 + z0


def source_at(i):
    zh, j = i // 8, lax.rem(i, 8)
    odd = lax.rem(j, 2)
    y = (1 - odd) * (j // 2) + odd * (7 - j // 2)
    return y * 4 + zh


def kernel(
    hidden_hbm, base_hbm, lora_in_hbm, lora_out_hbm, gain_hbm, keys_hbm, values_hbm, lengths_hbm,
    out_ref,
    hidden, base, lora_in, lora_out, gain, keys, values, lengths,
    slots, spread, merged,
    in_sems, send_dp, send_x, send_core, recv,
):
    dp, t = lax.axis_index("dp"), lax.axis_index("tensor")
    x, z_lo, core = t // 4, lax.rem(t // 2, 2), lax.rem(t, 2)
    x1, x0 = x // 2, lax.rem(x, 2)
    y2, y1, y0, z1, z0 = bits_of(dp)
    sibling = (dp, x * 4 + z_lo * 2 + (1 - core))
    x_partners = [(dp, lax.rem(x + d, 4) * 4 + z_lo * 2 + core) for d in (1, 3, 2)]
    dp_partners = [
        (index_of(flip(y2, core), flip(y1, f // 2), flip(y0, f % 2), flip(z1, x0), flip(z0, x1)), t) for f in range(4)
    ]
    own_class = jnp.logical_and(x == 0, core == 0)

    loads = []
    for i, (src, dst) in enumerate(
        (
            (lora_in_hbm, lora_in), (lora_out_hbm, lora_out), (hidden_hbm, hidden), (base_hbm, base),
            (keys_hbm, keys), (values_hbm, values), (gain_hbm, gain), (lengths_hbm, lengths),
        )
    ):
        load = pltpu.make_async_copy(src, dst, in_sems.at[i])
        load.start()
        loads.append(load)

    barrier = pltpu.get_barrier_semaphore()
    for f, partner in enumerate(dp_partners):
        if f == 0:
            @pl.when(jnp.logical_not(own_class))
            def _():
                pl.semaphore_signal(barrier, inc=1, device_id=partner, device_id_type=MESH)
        else:
            pl.semaphore_signal(barrier, inc=1, device_id=partner, device_id_type=MESH)
    for partner in x_partners + [sibling]:
        pl.semaphore_signal(barrier, inc=1, device_id=partner, device_id_type=MESH)

    loads[0].wait()
    loads[1].wait()
    rows = jnp.transpose(lora_in[...].astype(jnp.float32))
    packed = jnp.concatenate([rows[:PACKED], rows[PACKED:]], axis=1)
    ups = []
    for xi in range(4):
        even = lora_out[xi * 4 + z_lo * 2].astype(jnp.float32)
        odd = lora_out[xi * 4 + z_lo * 2 + 1].astype(jnp.float32)
        ups.append(jnp.concatenate([even, odd], axis=1))
    message = jnp.concatenate([ups[0], ups[1], packed, ups[2], ups[3]], axis=0)
    slots[dp] = message.astype(jnp.bfloat16)

    pl.semaphore_wait(barrier, jnp.where(own_class, 7, 8))

    def copy(slot, send_sem, partner):
        return pltpu.make_async_remote_copy(
            src_ref=slots.at[slot], dst_ref=slots.at[slot], send_sem=send_sem, recv_sem=recv.at[slot],
            device_id=partner, device_id_type=MESH,
        )

    for f, partner in enumerate(dp_partners):
        if f == 0:
            @pl.when(jnp.logical_not(own_class))
            def _():
                copy(dp, send_dp.at[f], partner).start()
        else:
            copy(dp, send_dp.at[f], partner).start()

    def roles(i):
        s = source_at(i)
        s2, _, _, sz1, sz0 = bits_of(s)
        same_core = flip(s2, y2) == core
        same_x = jnp.logical_and(flip(sz1, z1) == x0, flip(sz0, z0) == x1)
        same_core = jnp.logical_and(same_core, s != dp)
        return s, same_core, jnp.logical_and(same_core, same_x)

    def arrive(i, _):
        s, same_core, same_plane = roles(i)

        @pl.when(s != dp)
        def _():
            copy(s, send_core.at[s], sibling).wait_recv()

        @pl.when(same_plane)
        def _():
            for k, partner in enumerate(x_partners):
                copy(s, send_x.at[s * 3 + k], partner).start()

        @pl.when(same_core)
        def _():
            copy(s, send_core.at[s], sibling).start()

        return 0

    lax.fori_loop(0, N_DP, arrive, 0)

    group = slots[:, pl.ds((x // 2) * (SLOT - 16), 16), :].astype(jnp.float32)
    both = jnp.where(lax.rem(x, 2) == 0, group[:, :8], group[:, 8:]).reshape(256, 128)
    turned = pltpu.roll(both, 64, 1)
    lane = lax.broadcasted_iota(jnp.int32, (256, 128), 1)
    first = jnp.where(core == 0, both, turned)
    second = jnp.where(core == 0, turned, both)
    spread[:256] = jnp.where(lane < 64, first, 0.0).astype(jnp.bfloat16)
    spread[256:] = jnp.where(lane >= 64, second, 0.0).astype(jnp.bfloat16)

    loads[3].wait()

    def merge(s, _):
        update = lax.dot_general(
            slots[s, 16:16 + PACKED, :], spread[...], (((1,), (1,)), ((), ())), preferred_element_type=jnp.float32
        )
        for half in range(2):
            at = pl.ds(pl.multiple_of(s * 160 + half * PACKED, 16), PACKED)
            merged[at, :] = (base[at, :].astype(jnp.float32) + update[:, half * 256:half * 256 + 256]).astype(jnp.bfloat16)
        return 0

    lax.fori_loop(0, N_DP, merge, 0)

    loads[2].wait()
    query = jnp.dot(hidden[...], merged[...], preferred_element_type=jnp.float32)

    for i in (4, 5, 6, 7):
        loads[i].wait()
    gains = gain[...]
    heads = []
    for h in range(2):
        head = query[:, h * 128:h * 128 + 128]
        inverse = lax.rsqrt(jnp.mean(head * head, axis=-1, keepdims=True) + 1e-06)
        heads.append(head * inverse * gains)
    square = (32, 128)
    on_diagonal = lax.broadcasted_iota(jnp.int32, square, 0) == lax.broadcasted_iota(jnp.int32, square, 1)
    length_row = jnp.concatenate([lengths[...], jnp.zeros((1, 96), jnp.int32)], axis=1).astype(jnp.float32)
    length_column = jnp.sum(jnp.where(on_diagonal, length_row, 0.0), axis=1, keepdims=True).astype(jnp.int32)
    tile = (16, 512)
    row = lax.rem(lax.broadcasted_iota(jnp.int32, tile, 0), 8)
    column = lax.broadcasted_iota(jnp.int32, tile, 1)
    own_row = column // 64 == row
    position = lax.rem(column, 64)
    parts = []
    for j in range(4):
        normed = jnp.concatenate([heads[0][j * 8:j * 8 + 8], heads[1][j * 8:j * 8 + 8]], axis=0).astype(jnp.bfloat16)
        keys_tile = keys[j * 8:j * 8 + 8].reshape(512, 128)
        values_tile = values[j * 8:j * 8 + 8].reshape(512, 128)
        scores = lax.dot_general(
            normed, keys_tile, (((1,), (1,)), ((), ())), preferred_element_type=jnp.float32
        ) / math.sqrt(128)
        length = jnp.concatenate([length_column[j * 8:j * 8 + 8]] * 2, axis=0)
        scores = jnp.where(jnp.logical_and(own_row, position < length), scores, -jnp.inf)
        expo = jnp.exp(scores - jnp.max(scores, axis=-1, keepdims=True))
        weights = (expo / jnp.sum(expo, axis=-1, keepdims=True)).astype(jnp.bfloat16)
        parts.append(jnp.dot(weights, values_tile, preferred_element_type=jnp.float32))
    out_ref[...] = jnp.concatenate(
        [jnp.concatenate([part[h * 8:h * 8 + 8] for part in parts], axis=0) for h in range(2)], axis=1
    ).astype(jnp.bfloat16)

    for f, partner in enumerate(dp_partners):
        if f == 0:
            @pl.when(jnp.logical_not(own_class))
            def _():
                copy(dp, send_dp.at[f], partner).wait_send()
        else:
            copy(dp, send_dp.at[f], partner).wait_send()

    def sent(i, _):
        s, same_core, same_plane = roles(i)

        @pl.when(same_plane)
        def _():
            for k, partner in enumerate(x_partners):
                copy(s, send_x.at[s * 3 + k], partner).wait_send()

        @pl.when(same_core)
        def _():
            copy(s, send_core.at[s], sibling).wait_send()

        return 0

    lax.fori_loop(0, N_DP, sent, 0)


def local(
    hidden, query_base_matrix, input_side_factor, output_side_factor,
    query_norm_gain, cached_key_heads, cached_value_heads, lengths,
):
    bf16 = jnp.bfloat16
    return pl.pallas_call(
        kernel,
        out_shape=jax.ShapeDtypeStruct((32, 256), bf16),
        in_specs=[pl.BlockSpec(memory_space=pl.ANY)] * 8,
        out_specs=pl.BlockSpec(memory_space=pltpu.VMEM),
        scratch_shapes=[
            pltpu.VMEM((32, 5120), bf16),
            pltpu.VMEM((5120, 256), bf16),
            pltpu.VMEM((64, 160), bf16),
            pltpu.VMEM((16, 8, 64), bf16),
            pltpu.VMEM((1, 128), jnp.float32),
            pltpu.VMEM((32, 64, 128), bf16),
            pltpu.VMEM((32, 64, 128), bf16),
            pltpu.VMEM((1, 32), jnp.int32),
            pltpu.VMEM((N_DP, SLOT, 128), bf16),
            pltpu.VMEM((512, 128), bf16),
            pltpu.VMEM((5120, 256), bf16),
            pltpu.SemaphoreType.DMA((8,)),
            pltpu.SemaphoreType.DMA((4,)),
            pltpu.SemaphoreType.DMA((N_DP * 3,)),
            pltpu.SemaphoreType.DMA((N_DP,)),
            pltpu.SemaphoreType.DMA((N_DP,)),
        ],
        compiler_params=pltpu.CompilerParams(
            collective_id=0, has_side_effects=True, vmem_limit_bytes=56 * 2**20
        ),
        cost_estimate=pl.CostEstimate(flops=260_000_000, bytes_accessed=4_200_000, transcendentals=32768),
    )(
        hidden, query_base_matrix, input_side_factor.T, jnp.transpose(output_side_factor, (1, 2, 0)),
        query_norm_gain.reshape(1, 128), cached_key_heads.reshape(32, 64, 128),
        cached_value_heads.reshape(32, 64, 128), lengths.reshape(1, 32),
    )


def solution(mesh):
    in_specs = (
        P("dp", None),
        P(None, "tensor"),
        P("dp", None),
        P(None, None, "dp"),
        P(),
        P("dp", "tensor", None, None),
        P("dp", "tensor", None, None),
        P("dp"),
    )
    return jax.shard_map(local, mesh=mesh, in_specs=in_specs, out_specs=P("dp", "tensor"), check_vma=False)
```

time: 185 us -> 74.4 us (0.40)
  the two profiles are of different devices: /device:TPU:6 before, /device:TPU:256 now
where the time goes in v1:
time: 74.4 us; the launch traced here: 74.2 us
  Pallas kernels  72.9 us (98%)
  local copies, waits for them, and re-layouts  1.32 us (2%)
    pallas_call x1, Pallas kernels, local(): pl.pallas_call(kernel, out_shape=jax.ShapeDtypeStruct((32, 256), bf16), i...  72.9 us

profile of v1, /device:TPU:256, one launch (start us, length us, event | category | flops | bytes accessed | tf_op | source)
XLA Modules:
  0.0 74.2 jit_solution(918493167378956223)
XLA Ops:
  0.0 72.9 %shard_map.82 = bf16[32,256]{1,0:T(8,128)(2,1)} custom-call(bf16[32,5120]{1,0:T(8,128)(2,1)} %hidden_hbm.1, bf16[5120,256]{1,0:T(8,128)(2,1)} %base_hbm.1, bf16[64,160]{1,0:T(8,128)(2,1)} %bitcast.8, bf16[16,8,64]{2,1,0:T(8,128)(2,1)} %bitcast.9, f32[1,128]{1,0:T(1,128)} %bitcast.10, bf16[32,64,128]{2,1,0:T(8,128)(2,1)} %bitcast.6, ...), custom_call_target="tpu_custom_call" | custom-call | flops 260000000 | bytes 4200000 | tf_op jit(solution)/shard_map/pallas_call | solution.py:222
  72.9 1.3 %copy.10 = bf16[32,256]{1,0:T(8,128)(2,1)} copy(bf16[32,256]{1,0:T(8,128)(2,1)} %shard_map.82) | data formatting | bytes 32768

commit v2 on v1

--- a/solution.py
+++ b/solution.py
@@ -14,24 +14,28 @@
 SLOT = PACKED + 32
 
 
+ASSIGN = {"z1": "core"}
+BITS = ("y2", "y1", "y0", "z1", "z0")
+X_FLIPS = [f for f in (1, 3, 2) if not any(f >> i & 1 and f"x{i}" not in ASSIGN.values() for i in range(2))]
+FREE = [b for b in BITS if b not in ASSIGN]
+
+
 def flip(bit, other):
     return lax.rem(bit + other, 2)
 
 
-def bits_of(dp):
-    y, zh = dp // 4, lax.rem(dp, 4)
-    return y // 4, lax.rem(y // 2, 2), lax.rem(y, 2), zh // 2, lax.rem(zh, 2)
-
-
-def index_of(y2, y1, y0, z1, z0):
-    return y2 * 16 + y1 * 8 + y0 * 4 + z1 * 2 + z0
-
-
-def source_at(i):
-    zh, j = i // 8, lax.rem(i, 8)
-    odd = lax.rem(j, 2)
-    y = (1 - odd) * (j // 2) + odd * (7 - j // 2)
-    return y * 4 + zh
+def index_of(bits):
+    return bits["y2"] * 16 + bits["y1"] * 8 + bits["y0"] * 4 + bits["z1"] * 2 + bits["z0"]
+
+
+def sources(dp_bits, plane):
+    out = []
+    for f in range(2 ** len(FREE)):
+        bits = {}
+        for b in BITS:
+            bits[b] = flip(dp_bits[b], plane[ASSIGN[b]] if b in ASSIGN else f >> FREE.index(b) & 1)
+        out.append(index_of(bits))
+    return out
 
 
 def kernel(
@@ -43,14 +47,23 @@
 ):
     dp, t = lax.axis_index("dp"), lax.axis_index("tensor")
     x, z_lo, core = t // 4, lax.rem(t // 2, 2), lax.rem(t, 2)
-    x1, x0 = x // 2, lax.rem(x, 2)
-    y2, y1, y0, z1, z0 = bits_of(dp)
+    y, z_hi = dp // 4, lax.rem(dp, 4)
+    dp_bits = {"y2": y // 4, "y1": lax.rem(y // 2, 2), "y0": lax.rem(y, 2), "z1": z_hi // 2, "z0": lax.rem(z_hi, 2)}
     sibling = (dp, x * 4 + z_lo * 2 + (1 - core))
-    x_partners = [(dp, lax.rem(x + d, 4) * 4 + z_lo * 2 + core) for d in (1, 3, 2)]
-    dp_partners = [
-        (index_of(flip(y2, core), flip(y1, f // 2), flip(y0, f % 2), flip(z1, x0), flip(z0, x1)), t) for f in range(4)
-    ]
-    own_class = jnp.logical_and(x == 0, core == 0)
+
+    def plane(x_flip, core_flip):
+        return {
+            "x1": flip(x // 2, x_flip // 2), "x0": flip(lax.rem(x, 2), x_flip % 2), "core": flip(core, core_flip),
+        }
+
+    def x_partner(x_flip):
+        p = plane(x_flip, 0)
+        return (dp, (p["x1"] * 2 + p["x0"]) * 4 + z_lo * 2 + core)
+
+    x_partners = [x_partner(f) for f in X_FLIPS]
+    direct = sources(dp_bits, plane(0, 0))
+    by_x = [s for f in X_FLIPS for s in sources(dp_bits, plane(f, 0))]
+    by_core = [s for f in [0] + X_FLIPS for s in sources(dp_bits, plane(f, 1))]
 
     loads = []
     for i, (src, dst) in enumerate(
@@ -64,13 +77,10 @@
         loads.append(load)
 
     barrier = pltpu.get_barrier_semaphore()
-    for f, partner in enumerate(dp_partners):
-        if f == 0:
-            @pl.when(jnp.logical_not(own_class))
-            def _():
-                pl.semaphore_signal(barrier, inc=1, device_id=partner, device_id_type=MESH)
-        else:
-            pl.semaphore_signal(barrier, inc=1, device_id=partner, device_id_type=MESH)
+    for s in direct:
+        @pl.when(s != dp)
+        def _():
+            pl.semaphore_signal(barrier, inc=1, device_id=(s, t), device_id_type=MESH)
     for partner in x_partners + [sibling]:
         pl.semaphore_signal(barrier, inc=1, device_id=partner, device_id_type=MESH)
 
@@ -86,7 +96,8 @@
     message = jnp.concatenate([ups[0], ups[1], packed, ups[2], ups[3]], axis=0)
     slots[dp] = message.astype(jnp.bfloat16)
 
-    pl.semaphore_wait(barrier, jnp.where(own_class, 7, 8))
+    n_partners = len(direct) + len(x_partners) + 1
+    pl.semaphore_wait(barrier, jnp.where(direct[0] == dp, n_partners - 1, n_partners))
 
     def copy(slot, send_sem, partner):
         return pltpu.make_async_remote_copy(
@@ -94,63 +105,52 @@
             device_id=partner, device_id_type=MESH,
         )
 
-    for f, partner in enumerate(dp_partners):
-        if f == 0:
-            @pl.when(jnp.logical_not(own_class))
-            def _():
-                copy(dp, send_dp.at[f], partner).start()
-        else:
-            copy(dp, send_dp.at[f], partner).start()
-
-    def roles(i):
-        s = source_at(i)
-        s2, _, _, sz1, sz0 = bits_of(s)
-        same_core = flip(s2, y2) == core
-        same_x = jnp.logical_and(flip(sz1, z1) == x0, flip(sz0, z0) == x1)
-        same_core = jnp.logical_and(same_core, s != dp)
-        return s, same_core, jnp.logical_and(same_core, same_x)
-
-    def arrive(i, _):
-        s, same_core, same_plane = roles(i)
-
-        @pl.when(s != dp)
-        def _():
-            copy(s, send_core.at[s], sibling).wait_recv()
-
-        @pl.when(same_plane)
-        def _():
+    n_direct, n_x = len(direct), len(x_partners)
+    for i, s in enumerate(direct):
+        @pl.when(s != dp)
+        def _():
+            copy(dp, send_dp.at[i], (s, t)).start()
+
+    for i, s in enumerate(direct):
+        @pl.when(s != dp)
+        def _():
+            copy(s, send_core.at[i], sibling).wait_recv()
             for k, partner in enumerate(x_partners):
-                copy(s, send_x.at[s * 3 + k], partner).start()
-
-        @pl.when(same_core)
-        def _():
-            copy(s, send_core.at[s], sibling).start()
-
-        return 0
-
-    lax.fori_loop(0, N_DP, arrive, 0)
+                copy(s, send_x.at[i * n_x + k], partner).start()
+            copy(s, send_core.at[i], sibling).start()
+
+    for i, s in enumerate(by_x):
+        @pl.when(s != dp)
+        def _():
+            copy(s, send_core.at[n_direct + i], sibling).wait_recv()
+            copy(s, send_core.at[n_direct + i], sibling).start()
+
+    for s in by_core:
+        @pl.when(s != dp)
+        def _():
+            copy(s, send_core.at[0], sibling).wait_recv()
 
     group = slots[:, pl.ds((x // 2) * (SLOT - 16), 16), :].astype(jnp.float32)
     both = jnp.where(lax.rem(x, 2) == 0, group[:, :8], group[:, 8:]).reshape(256, 128)
     turned = pltpu.roll(both, 64, 1)
-    lane = lax.broadcasted_iota(jnp.int32, (256, 128), 1)
-    first = jnp.where(core == 0, both, turned)
-    second = jnp.where(core == 0, turned, both)
-    spread[:256] = jnp.where(lane < 64, first, 0.0).astype(jnp.bfloat16)
-    spread[256:] = jnp.where(lane >= 64, second, 0.0).astype(jnp.bfloat16)
+    lane = lax.broadcasted_iota(jnp.int32, (128, 256), 0)
+    first = jnp.transpose(jnp.where(core == 0, both, turned))
+    second = jnp.transpose(jnp.where(core == 0, turned, both))
+    spread[:, :256] = jnp.where(lane < 64, first, 0.0).astype(jnp.bfloat16)
+    spread[:, 256:] = jnp.where(lane >= 64, second, 0.0).astype(jnp.bfloat16)
 
     loads[3].wait()
 
     def merge(s, _):
         update = lax.dot_general(
-            slots[s, 16:16 + PACKED, :], spread[...], (((1,), (1,)), ((), ())), preferred_element_type=jnp.float32
+            slots[s, 16:16 + PACKED, :], spread[...], (((1,), (0,)), ((), ())), preferred_element_type=jnp.float32
         )
         for half in range(2):
             at = pl.ds(pl.multiple_of(s * 160 + half * PACKED, 16), PACKED)
             merged[at, :] = (base[at, :].astype(jnp.float32) + update[:, half * 256:half * 256 + 256]).astype(jnp.bfloat16)
         return 0
 
-    lax.fori_loop(0, N_DP, merge, 0)
+    lax.fori_loop(0, N_DP, merge, 0, unroll=True)
 
     loads[2].wait()
     query = jnp.dot(hidden[...], merged[...], preferred_element_type=jnp.float32)
@@ -189,29 +189,18 @@
         [jnp.concatenate([part[h * 8:h * 8 + 8] for part in parts], axis=0) for h in range(2)], axis=1
     ).astype(jnp.bfloat16)
 
-    for f, partner in enumerate(dp_partners):
-        if f == 0:
-            @pl.when(jnp.logical_not(own_class))
-            def _():
-                copy(dp, send_dp.at[f], partner).wait_send()
-        else:
-            copy(dp, send_dp.at[f], partner).wait_send()
-
-    def sent(i, _):
-        s, same_core, same_plane = roles(i)
-
-        @pl.when(same_plane)
-        def _():
+    for i, s in enumerate(direct):
+        @pl.when(s != dp)
+        def _():
+            copy(dp, send_dp.at[i], (s, t)).wait_send()
             for k, partner in enumerate(x_partners):
-                copy(s, send_x.at[s * 3 + k], partner).wait_send()
-
-        @pl.when(same_core)
-        def _():
-            copy(s, send_core.at[s], sibling).wait_send()
-
-        return 0
-
-    lax.fori_loop(0, N_DP, sent, 0)
+                copy(s, send_x.at[i * n_x + k], partner).wait_send()
+            copy(s, send_core.at[i], sibling).wait_send()
+
+    for i, s in enumerate(by_x):
+        @pl.when(s != dp)
+        def _():
+            copy(s, send_core.at[n_direct + i], sibling).wait_send()
 
 
 def local(
@@ -234,10 +223,10 @@
             pltpu.VMEM((32, 64, 128), bf16),
             pltpu.VMEM((1, 32), jnp.int32),
             pltpu.VMEM((N_DP, SLOT, 128), bf16),
-            pltpu.VMEM((512, 128), bf16),
+            pltpu.VMEM((128, 512), bf16),
             pltpu.VMEM((5120, 256), bf16),
             pltpu.SemaphoreType.DMA((8,)),
-            pltpu.SemaphoreType.DMA((4,)),
+            pltpu.SemaphoreType.DMA((N_DP,)),
             pltpu.SemaphoreType.DMA((N_DP * 3,)),
             pltpu.SemaphoreType.DMA((N_DP,)),
             pltpu.SemaphoreType.DMA((N_DP,)),

time: 74.4 us -> 32.6 us (0.44)
  the two profiles are of different devices: /device:TPU:256 before, /device:TPU:70 now
where the time goes in v2:
time: 32.6 us; the launch traced here: 32.4 us
  Pallas kernels  31 us (95%)
  local copies, waits for them, and re-layouts  1.32 us (4%)
    pallas_call x1, Pallas kernels, local(): pl.pallas_call(kernel, out_shape=jax.ShapeDtypeStruct((32, 256), bf16), i...  31 us
    unnamed x1, local copies, waits for them, and re-layouts  1.32 us

profile of v2, /device:TPU:70, one launch (start us, length us, event | category | flops | bytes accessed | tf_op | source)
XLA Modules:
  0.0 32.4 jit_solution(9064331744685585085)
XLA Ops:
  0.0 31.0 %shard_map.82 = bf16[32,256]{1,0:T(8,128)(2,1)} custom-call(bf16[32,5120]{1,0:T(8,128)(2,1)} %hidden_hbm.1, bf16[5120,256]{1,0:T(8,128)(2,1)} %base_hbm.1, bf16[64,160]{1,0:T(8,128)(2,1)} %bitcast.8, bf16[16,8,64]{2,1,0:T(8,128)(2,1)} %bitcast.9, f32[1,128]{1,0:T(1,128)} %bitcast.10, bf16[32,64,128]{2,1,0:T(8,128)(2,1)} %bitcast.6, ...), custom_call_target="tpu_custom_call" | custom-call | flops 260000000 | bytes 4200000 | tf_op jit(solution)/shard_map/pallas_call | solution.py:211
  31.0 1.3 %copy.10 = bf16[32,256]{1,0:T(8,128)(2,1)} copy(bf16[32,256]{1,0:T(8,128)(2,1)} %shard_map.82) | data formatting | bytes 32768

commit v3 on v2

v3 whole, which is shorter than its diff:
```python
import functools
import math

import jax
import jax.numpy as jnp
from jax import lax
from jax.experimental import pallas as pl
from jax.experimental.pallas import tpu as pltpu
from jax.sharding import PartitionSpec as P

MESH = pl.DeviceIdType.MESH
N_DP = 32
PACKED = 80
GROUP = 16
SENT = GROUP + PACKED
SLOT = SENT + GROUP
SERVE_Y = (0, 1, 2, 3, 7, 6, 5, 4)
AWAIT_Y = (0, 1, 7, 2, 6, 3, 5, 4)


def flip(bit, other):
    return lax.rem(bit + other, 2)


def kernel(
    hidden_hbm, base_hbm, lora_in_hbm, lora_out_hbm, gain_hbm, keys_hbm, values_hbm, lengths_hbm,
    out_ref,
    hidden, base, lora_in, lora_out, gain, keys, values, lengths,
    slots, spread, merged,
    in_sems, send_dp, send_core, recv,
):
    dp, t = lax.axis_index("dp"), lax.axis_index("tensor")
    x, z_lo, core = t // 4, lax.rem(t // 2, 2), lax.rem(t, 2)
    z1, z0 = lax.rem(dp // 2, 2), lax.rem(dp, 2)
    sibling = (dp, x * 4 + z_lo * 2 + (1 - core))
    reach = flip(z1, core)

    def partner(y, far):
        swap = core * (1 - flip(z0, far))
        return (y * 4 + reach * 2 + far, x * 4 + flip(z_lo, swap) * 2 + core)

    serve = [partner(y, far) for far in range(2) for y in SERVE_Y]
    direct = [partner(y, far)[0] for far in range(2) for y in AWAIT_Y]
    by_core = [y * 4 + (1 - reach) * 2 + far for far in range(2) for y in AWAIT_Y]

    def load(i):
        src, dst = (
            (lora_in_hbm, lora_in), (lora_out_hbm, lora_out), (hidden_hbm, hidden), (base_hbm, base),
            (keys_hbm, keys), (values_hbm, values), (gain_hbm, gain), (lengths_hbm, lengths),
        )[i]
        return pltpu.make_async_copy(src, dst, in_sems.at[i])

    for i in (0, 1):
        load(i).start()

    barrier = pltpu.get_barrier_semaphore()
    for device in serve:
        @pl.when(device[0] != dp)
        def _():
            pl.semaphore_signal(barrier, inc=1, device_id=device, device_id_type=MESH)
    pl.semaphore_signal(barrier, inc=1, device_id=sibling, device_id_type=MESH)

    load(0).wait()
    load(1).wait()
    rows = jnp.transpose(lora_in[...].astype(jnp.float32))
    packed = jnp.concatenate([rows[:PACKED], rows[PACKED:]], axis=1)
    slots[dp, GROUP:SENT, :] = packed.astype(jnp.bfloat16)
    for group in range(2):
        even = lora_out[x * 4 + group * 2].astype(jnp.float32)
        odd = lora_out[x * 4 + group * 2 + 1].astype(jnp.float32)
        columns = jnp.concatenate([jnp.concatenate([even, odd], axis=1)] * 2, axis=0)
        slots[dp, group * SENT:group * SENT + GROUP, :] = columns.astype(jnp.bfloat16)

    pl.semaphore_wait(barrier, jnp.where(core == 0, 16, 17))

    def copy(slot, send_sem, device):
        group = lax.rem(device[1] // 2, 2)
        rows = pl.ds(pl.multiple_of(group * GROUP, GROUP), SENT)
        return pltpu.make_async_remote_copy(
            src_ref=slots.at[slot, rows], dst_ref=slots.at[slot, rows], send_sem=send_sem, recv_sem=recv.at[slot],
            device_id=device, device_id_type=MESH,
        )

    for i, device in enumerate(serve):
        @pl.when(device[0] != dp)
        def _():
            copy(dp, send_dp.at[i], device).start()

    for i in range(2, 8):
        load(i).start()

    for i, s in enumerate(direct):
        @pl.when(s != dp)
        def _():
            copy(s, send_core.at[i], sibling).wait_recv()
            copy(s, send_core.at[i], sibling).start()

    for s in by_core:
        @pl.when(s != dp)
        def _():
            copy(s, send_core.at[0], sibling).wait_recv()

    group = slots[:, pl.ds(pl.multiple_of(z_lo * SENT, GROUP), GROUP), :].astype(jnp.float32)
    both = group[:, :8].reshape(256, 128)
    turned = pltpu.roll(both, 64, 1)
    lane = lax.broadcasted_iota(jnp.int32, (128, 256), 0)
    first = jnp.transpose(jnp.where(core == 0, both, turned))
    second = jnp.transpose(jnp.where(core == 0, turned, both))
    spread[:, :256] = jnp.where(lane < 64, first, 0.0).astype(jnp.bfloat16)
    spread[:, 256:] = jnp.where(lane >= 64, second, 0.0).astype(jnp.bfloat16)

    load(3).wait()

    def merge(s, _):
        update = lax.dot_general(
            slots[s, GROUP:SENT, :], spread[...], (((1,), (0,)), ((), ())), preferred_element_type=jnp.float32
        )
        for half in range(2):
            at = pl.ds(pl.multiple_of(s * 160 + half * PACKED, 16), PACKED)
            merged[at, :] = (base[at, :].astype(jnp.float32) + update[:, half * 256:half * 256 + 256]).astype(jnp.bfloat16)
        return 0

    lax.fori_loop(0, N_DP, merge, 0, unroll=True)

    load(2).wait()
    query = jnp.dot(hidden[...], merged[...], preferred_element_type=jnp.float32)

    for i in (4, 5, 6, 7):
        load(i).wait()
    gains = gain[...]
    heads = []
    for h in range(2):
        head = query[:, h * 128:h * 128 + 128]
        inverse = lax.rsqrt(jnp.mean(head * head, axis=-1, keepdims=True) + 1e-06)
        heads.append(head * inverse * gains)
    square = (32, 128)
    on_diagonal = lax.broadcasted_iota(jnp.int32, square, 0) == lax.broadcasted_iota(jnp.int32, square, 1)
    length_row = jnp.concatenate([lengths[...], jnp.zeros((1, 96), jnp.int32)], axis=1).astype(jnp.float32)
    length_column = jnp.sum(jnp.where(on_diagonal, length_row, 0.0), axis=1, keepdims=True).astype(jnp.int32)
    tile = (16, 512)
    row = lax.rem(lax.broadcasted_iota(jnp.int32, tile, 0), 8)
    column = lax.broadcasted_iota(jnp.int32, tile, 1)
    own_row = column // 64 == row
    position = lax.rem(column, 64)
    parts = []
    for j in range(4):
        normed = jnp.concatenate([heads[0][j * 8:j * 8 + 8], heads[1][j * 8:j * 8 + 8]], axis=0).astype(jnp.bfloat16)
        keys_tile = keys[j * 8:j * 8 + 8].reshape(512, 128)
        values_tile = values[j * 8:j * 8 + 8].reshape(512, 128)
        scores = lax.dot_general(
            normed, keys_tile, (((1,), (1,)), ((), ())), preferred_element_type=jnp.float32
        ) / math.sqrt(128)
        length = jnp.concatenate([length_column[j * 8:j * 8 + 8]] * 2, axis=0)
        scores = jnp.where(jnp.logical_and(own_row, position < length), scores, -jnp.inf)
        expo = jnp.exp(scores - jnp.max(scores, axis=-1, keepdims=True))
        weights = (expo * (1.0 / jnp.sum(expo, axis=-1, keepdims=True))).astype(jnp.bfloat16)
        parts.append(jnp.dot(weights, values_tile, preferred_element_type=jnp.float32))
    out_ref[...] = jnp.concatenate(
        [jnp.concatenate([part[h * 8:h * 8 + 8] for part in parts], axis=0) for h in range(2)], axis=1
    ).astype(jnp.bfloat16)

    for i, device in enumerate(serve):
        @pl.when(device[0] != dp)
        def _():
            copy(dp, send_dp.at[i], device).wait_send()

    for i, s in enumerate(direct):
        @pl.when(s != dp)
        def _():
            copy(s, send_core.at[i], sibling).wait_send()


def local(
    hidden, query_base_matrix, input_side_factor, output_side_factor,
    query_norm_gain, cached_key_heads, cached_value_heads, lengths,
):
    bf16 = jnp.bfloat16
    return pl.pallas_call(
        kernel,
        out_shape=jax.ShapeDtypeStruct((32, 256), bf16),
        in_specs=[pl.BlockSpec(memory_space=pl.ANY)] * 8,
        out_specs=pl.BlockSpec(memory_space=pltpu.VMEM),
        scratch_shapes=[
            pltpu.VMEM((32, 5120), bf16),
            pltpu.VMEM((5120, 256), bf16),
            pltpu.VMEM((64, 160), bf16),
            pltpu.VMEM((16, 8, 64), bf16),
            pltpu.VMEM((1, 128), jnp.float32),
            pltpu.VMEM((32, 64, 128), bf16),
            pltpu.VMEM((32, 64, 128), bf16),
            pltpu.VMEM((1, 32), jnp.int32),
            pltpu.VMEM((N_DP, SLOT, 128), bf16),
            pltpu.VMEM((128, 512), bf16),
            pltpu.VMEM((5120, 256), bf16),
            pltpu.SemaphoreType.DMA((8,)),
            pltpu.SemaphoreType.DMA((16,)),
            pltpu.SemaphoreType.DMA((16,)),
            pltpu.SemaphoreType.DMA((N_DP,)),
        ],
        compiler_params=pltpu.CompilerParams(
            collective_id=0, has_side_effects=True, vmem_limit_bytes=56 * 2**20
        ),
        cost_estimate=pl.CostEstimate(flops=260_000_000, bytes_accessed=4_200_000, transcendentals=32768),
    )(
        hidden, query_base_matrix, input_side_factor.T, jnp.transpose(output_side_factor, (1, 2, 0)),
        query_norm_gain.reshape(1, 128), cached_key_heads.reshape(32, 64, 128),
        cached_value_heads.reshape(32, 64, 128), lengths.reshape(1, 32),
    )


def solution(mesh):
    in_specs = (
        P("dp", None),
        P(None, "tensor"),
        P("dp", None),
        P(None, None, "dp"),
        P(),
        P("dp", "tensor", None, None),
        P("dp", "tensor", None, None),
        P("dp"),
    )
    return jax.shard_map(local, mesh=mesh, in_specs=in_specs, out_specs=P("dp", "tensor"), check_vma=False)
```

time: 32.6 us -> 29.8 us (0.914)
  the two profiles are of different devices: /device:TPU:70 before, /device:TPU:1 now
where the time goes in v3:
time: 29.8 us; the launch traced here: 29.6 us
  Pallas kernels  28.2 us (95%)
  local copies, waits for them, and re-layouts  1.32 us (4%)
    pallas_call x1, Pallas kernels, local(): pl.pallas_call(kernel, out_shape=jax.ShapeDtypeStruct((32, 256), bf16), i...  28.2 us
    unnamed x1, local copies, waits for them, and re-layouts  1.32 us

profile of v3, /device:TPU:1, one launch (start us, length us, event | category | flops | bytes accessed | tf_op | source)
XLA Modules:
  0.0 29.6 jit_solution(5183726690555662889)
XLA Ops:
  0.0 28.2 %shard_map.82 = bf16[32,256]{1,0:T(8,128)(2,1)} custom-call(bf16[32,5120]{1,0:T(8,128)(2,1)} %hidden_hbm.1, bf16[5120,256]{1,0:T(8,128)(2,1)} %base_hbm.1, bf16[64,160]{1,0:T(8,128)(2,1)} %bitcast.8, bf16[16,8,64]{2,1,0:T(8,128)(2,1)} %bitcast.9, f32[1,128]{1,0:T(1,128)} %bitcast.10, bf16[32,64,128]{2,1,0:T(8,128)(2,1)} %bitcast.6, ...), custom_call_target="tpu_custom_call" | custom-call | flops 260000000 | bytes 4200000 | tf_op jit(solution)/shard_map/pallas_call | solution.py:178
  28.3 1.3 %copy.10 = bf16[32,256]{1,0:T(8,128)(2,1)} copy(bf16[32,256]{1,0:T(8,128)(2,1)} %shard_map.82) | data formatting | bytes 32768

commit v4 on v3

--- a/solution.py
+++ b/solution.py
@@ -12,10 +12,8 @@
 N_DP = 32
 PACKED = 80
 GROUP = 16
-SENT = GROUP + PACKED
-SLOT = SENT + GROUP
-SERVE_Y = (0, 1, 2, 3, 7, 6, 5, 4)
-AWAIT_Y = (0, 1, 7, 2, 6, 3, 5, 4)
+X_FLIPS = (2, 1, 3)
+UPPER_Y = (0, 1, 3, 2)
 
 
 def flip(bit, other):
@@ -26,22 +24,30 @@
     hidden_hbm, base_hbm, lora_in_hbm, lora_out_hbm, gain_hbm, keys_hbm, values_hbm, lengths_hbm,
     out_ref,
     hidden, base, lora_in, lora_out, gain, keys, values, lengths,
-    slots, spread, merged,
-    in_sems, send_dp, send_core, recv,
+    slots, ups, own_ups, spread, merged,
+    in_sems, send_dp, send_x, send_core, recv,
 ):
     dp, t = lax.axis_index("dp"), lax.axis_index("tensor")
     x, z_lo, core = t // 4, lax.rem(t // 2, 2), lax.rem(t, 2)
     z1, z0 = lax.rem(dp // 2, 2), lax.rem(dp, 2)
     sibling = (dp, x * 4 + z_lo * 2 + (1 - core))
+    y0, x1, x0 = lax.rem(dp // 4, 2), x // 2, lax.rem(x, 2)
+    early, late = z1 == 0, z1 == 1
+    sender = jnp.logical_and(late, core == 1)
+    taker = jnp.logical_not(sender)
+    both_halves = jnp.logical_and(late, core == 0)
     reach = flip(z1, core)
 
-    def partner(y, far):
-        swap = core * (1 - flip(z0, far))
-        return (y * 4 + reach * 2 + far, x * 4 + flip(z_lo, swap) * 2 + core)
-
-    serve = [partner(y, far) for far in range(2) for y in SERVE_Y]
-    direct = [partner(y, far)[0] for far in range(2) for y in AWAIT_Y]
-    by_core = [y * 4 + (1 - reach) * 2 + far for far in range(2) for y in AWAIT_Y]
+    def shards(half, x_flip):
+        odd, z = flip(y0, flip(x1, x_flip // 2)), flip(z0, flip(x0, x_flip % 2))
+        return [(upper * 2 + odd) * 4 + half * 2 + z for upper in UPPER_Y]
+
+    def devices(half, to_core):
+        swap = flip(z1, half) * (1 - x0)
+        return [(s, x * 4 + flip(z_lo, swap) * 2 + to_core) for s in shards(half, 0)]
+
+    x_partners = [(dp, (flip(x1, f // 2) * 2 + flip(x0, f % 2)) * 4 + z_lo * 2 + core) for f in X_FLIPS]
+    serve = devices(reach, core * z1)
 
     def load(i):
         src, dst = (
@@ -54,54 +60,144 @@
         load(i).start()
 
     barrier = pltpu.get_barrier_semaphore()
-    for device in serve:
-        @pl.when(device[0] != dp)
-        def _():
-            pl.semaphore_signal(barrier, inc=1, device_id=device, device_id_type=MESH)
-    pl.semaphore_signal(barrier, inc=1, device_id=sibling, device_id_type=MESH)
+
+    def signal(device):
+        pl.semaphore_signal(barrier, inc=1, device_id=device, device_id_type=MESH)
+
+    @pl.when(taker)
+    def _():
+        for device in devices(reach, core):
+            @pl.when(device[0] != dp)
+            def _():
+                signal(device)
+        for device in x_partners:
+            signal(device)
+
+    @pl.when(both_halves)
+    def _():
+        for device in devices(0, 1):
+            signal(device)
+
+    @pl.when(jnp.logical_not(both_halves))
+    def _():
+        signal(sibling)
+
+    @pl.when(early)
+    def _():
+        for i in range(2, 8):
+            load(i).start()
 
     load(0).wait()
     load(1).wait()
     rows = jnp.transpose(lora_in[...].astype(jnp.float32))
     packed = jnp.concatenate([rows[:PACKED], rows[PACKED:]], axis=1)
-    slots[dp, GROUP:SENT, :] = packed.astype(jnp.bfloat16)
+    slots[dp] = packed.astype(jnp.bfloat16)
     for group in range(2):
-        even = lora_out[x * 4 + group * 2].astype(jnp.float32)
-        odd = lora_out[x * 4 + group * 2 + 1].astype(jnp.float32)
-        columns = jnp.concatenate([jnp.concatenate([even, odd], axis=1)] * 2, axis=0)
-        slots[dp, group * SENT:group * SENT + GROUP, :] = columns.astype(jnp.bfloat16)
-
-    pl.semaphore_wait(barrier, jnp.where(core == 0, 16, 17))
-
-    def copy(slot, send_sem, device):
-        group = lax.rem(device[1] // 2, 2)
-        rows = pl.ds(pl.multiple_of(group * GROUP, GROUP), SENT)
+        rows = []
+        for xi in range(4):
+            even = lora_out[xi * 4 + group * 2].astype(jnp.float32)
+            odd = lora_out[xi * 4 + group * 2 + 1].astype(jnp.float32)
+            rows.append(jnp.concatenate([even, odd], axis=1))
+        own_ups[group] = jnp.concatenate(rows, axis=0).astype(jnp.bfloat16)
+    ups[dp] = own_ups[z_lo]
+
+    own_class = jnp.logical_and(x == 0, core == 0)
+    pl.semaphore_wait(barrier, jnp.where(sender, 4, jnp.where(own_class, 7, 8)))
+
+    def remote(src, dst, send_sem, recv_sem, device):
         return pltpu.make_async_remote_copy(
-            src_ref=slots.at[slot, rows], dst_ref=slots.at[slot, rows], send_sem=send_sem, recv_sem=recv.at[slot],
-            device_id=device, device_id_type=MESH,
+            src_ref=src, dst_ref=dst, send_sem=send_sem, recv_sem=recv_sem, device_id=device, device_id_type=MESH
         )
 
-    for i, device in enumerate(serve):
-        @pl.when(device[0] != dp)
+    def down(s, send_sem, device):
+        return remote(slots.at[s], slots.at[s], send_sem.at[0], recv.at[0, s], device)
+
+    def own_up(send_sem, device):
+        z_lo_there = lax.rem(device[1] // 2, 2)
+        return remote(own_ups.at[z_lo_there], ups.at[dp], send_sem.at[1], recv.at[1, dp], device)
+
+    def up(s, send_sem, device):
+        rows = pl.ds(pl.multiple_of(device[1] // 8 * GROUP, GROUP), GROUP)
+        return remote(ups.at[s, rows], ups.at[s, rows], send_sem.at[1], recv.at[1, s], device)
+
+    def serve_each(act):
+        for i, device in enumerate(serve):
+            @pl.when(device[0] != dp)
+            def _():
+                act(send_dp.at[i], device)
+
+    serve_each(lambda sem, device: own_up(sem, device).start())
+    serve_each(lambda sem, device: down(dp, sem, device).start())
+
+    @pl.when(late)
+    def _():
+        for i in range(2, 8):
+            load(i).start()
+
+    def each(half, x_flips, act):
+        for j, f in enumerate(x_flips):
+            for i, s in enumerate(shards(half, f)):
+                @pl.when(s != dp)
+                def _():
+                    act(s, j * 4 + i)
+
+    def halves(act):
+        @pl.when(taker)
         def _():
-            copy(dp, send_dp.at[i], device).start()
-
-    for i in range(2, 8):
-        load(i).start()
-
-    for i, s in enumerate(direct):
-        @pl.when(s != dp)
+            act(reach, 0)
+
+        @pl.when(both_halves)
         def _():
-            copy(s, send_core.at[i], sibling).wait_recv()
-            copy(s, send_core.at[i], sibling).start()
-
-    for s in by_core:
-        @pl.when(s != dp)
+            act(0, 1)
+
+    def take(kind, arrival):
+        def take_half(half, n):
+            def act(s, i):
+                arrival(s).wait_recv()
+                for k, device in enumerate(x_partners):
+                    kind(s, send_x.at[n * 12 + i * 3 + k], device).start()
+                kind(s, send_core.at[n * 16 + i], sibling).start()
+
+            each(half, (0,), act)
+
+        halves(take_half)
+
+    def pass_on(kind):
+        def pass_half(half, n):
+            def act(s, i):
+                kind(s, send_core.at[0], sibling).wait_recv()
+                kind(s, send_core.at[n * 16 + 4 + i], sibling).start()
+
+            each(half, X_FLIPS, act)
+
+        halves(pass_half)
+
+    def from_sibling(kind):
+        def wait_half(half):
+            for i in range(16):
+                s = (i // 2) * 4 + half * 2 + i % 2
+
+                @pl.when(s != dp)
+                def _():
+                    kind(s, send_core.at[0], sibling).wait_recv()
+
+        @pl.when(jnp.logical_not(both_halves))
         def _():
-            copy(s, send_core.at[0], sibling).wait_recv()
-
-    group = slots[:, pl.ds(pl.multiple_of(z_lo * SENT, GROUP), GROUP), :].astype(jnp.float32)
-    both = group[:, :8].reshape(256, 128)
+            wait_half(1 - reach)
+
+        @pl.when(sender)
+        def _():
+            wait_half(reach)
+
+    take(up, lambda s: remote(own_ups.at[z_lo], ups.at[s], send_dp.at[0, 1], recv.at[1, s], sibling))
+    take(down, lambda s: down(s, send_core.at[0], sibling))
+    pass_on(up)
+    pass_on(down)
+    from_sibling(up)
+    from_sibling(down)
+
+    pair = ups[:, pl.ds(pl.multiple_of(x1 * GROUP, GROUP), GROUP), :].astype(jnp.float32)
+    both = jnp.where(x0 == 0, pair[:, :8], pair[:, 8:]).reshape(256, 128)
     turned = pltpu.roll(both, 64, 1)
     lane = lax.broadcasted_iota(jnp.int32, (128, 256), 0)
     first = jnp.transpose(jnp.where(core == 0, both, turned))
@@ -113,7 +209,7 @@
 
     def merge(s, _):
         update = lax.dot_general(
-            slots[s, GROUP:SENT, :], spread[...], (((1,), (0,)), ((), ())), preferred_element_type=jnp.float32
+            slots[s], spread[...], (((1,), (0,)), ((), ())), preferred_element_type=jnp.float32
         )
         for half in range(2):
             at = pl.ds(pl.multiple_of(s * 160 + half * PACKED, 16), PACKED)
@@ -159,15 +255,23 @@
         [jnp.concatenate([part[h * 8:h * 8 + 8] for part in parts], axis=0) for h in range(2)], axis=1
     ).astype(jnp.bfloat16)
 
-    for i, device in enumerate(serve):
-        @pl.when(device[0] != dp)
-        def _():
-            copy(dp, send_dp.at[i], device).wait_send()
-
-    for i, s in enumerate(direct):
-        @pl.when(s != dp)
-        def _():
-            copy(s, send_core.at[i], sibling).wait_send()
+    serve_each(lambda sem, device: own_up(sem, device).wait_send())
+    serve_each(lambda sem, device: down(dp, sem, device).wait_send())
+
+    def sent(half, n):
+        def direct(s, i):
+            for k, device in enumerate(x_partners):
+                for kind in (up, down):
+                    kind(s, send_x.at[n * 12 + i * 3 + k], device).wait_send()
+
+        def every(s, i):
+            for kind in (up, down):
+                kind(s, send_core.at[n * 16 + i], sibling).wait_send()
+
+        each(half, (0,), direct)
+        each(half, (0,) + X_FLIPS, every)
+
+    halves(sent)
 
 
 def local(
@@ -189,13 +293,16 @@
             pltpu.VMEM((32, 64, 128), bf16),
             pltpu.VMEM((32, 64, 128), bf16),
             pltpu.VMEM((1, 32), jnp.int32),
-            pltpu.VMEM((N_DP, SLOT, 128), bf16),
+            pltpu.VMEM((N_DP, PACKED, 128), bf16),
+            pltpu.VMEM((N_DP, 2 * GROUP, 128), bf16),
+            pltpu.VMEM((2, 2 * GROUP, 128), bf16),
             pltpu.VMEM((128, 512), bf16),
             pltpu.VMEM((5120, 256), bf16),
             pltpu.SemaphoreType.DMA((8,)),
-            pltpu.SemaphoreType.DMA((16,)),
-            pltpu.SemaphoreType.DMA((16,)),
-            pltpu.SemaphoreType.DMA((N_DP,)),
+            pltpu.SemaphoreType.DMA((4, 2)),
+            pltpu.SemaphoreType.DMA((24, 2)),
+            pltpu.SemaphoreType.DMA((32, 2)),
+            pltpu.SemaphoreType.DMA((2, N_DP)),
         ],
         compiler_params=pltpu.CompilerParams(
             collective_id=0, has_side_effects=True, vmem_limit_bytes=56 * 2**20

time: 29.8 us -> 30.7 us (1.030)
  the two profiles are of different devices: /device:TPU:1 before, /device:TPU:257 now
where the time goes in v4:
time: 30.7 us; the launch traced here: 30.5 us
  Pallas kernels  29.1 us (95%)
  local copies, waits for them, and re-layouts  1.32 us (4%)
    pallas_call x1, Pallas kernels, local(): pl.pallas_call(kernel, out_shape=jax.ShapeDtypeStruct((32, 256), bf16), i...  29.1 us
    unnamed x1, local copies, waits for them, and re-layouts  1.32 us

profile of v4, /device:TPU:257, one launch (start us, length us, event | category | flops | bytes accessed | tf_op | source)
XLA Modules:
  0.0 30.5 jit_solution(15683142580189087055)
XLA Ops:
  0.0 29.1 %shard_map.82 = bf16[32,256]{1,0:T(8,128)(2,1)} custom-call(bf16[32,5120]{1,0:T(8,128)(2,1)} %hidden_hbm.1, bf16[5120,256]{1,0:T(8,128)(2,1)} %base_hbm.1, bf16[64,160]{1,0:T(8,128)(2,1)} %bitcast.8, bf16[16,8,64]{2,1,0:T(8,128)(2,1)} %bitcast.9, f32[1,128]{1,0:T(1,128)} %bitcast.10, bf16[32,64,128]{2,1,0:T(8,128)(2,1)} %bitcast.6, ...), custom_call_target="tpu_custom_call" | custom-call | flops 260000000 | bytes 4200000 | tf_op jit(solution)/shard_map/pallas_call | solution.py:282
  29.1 1.3 %copy.10 = bf16[32,256]{1,0:T(8,128)(2,1)} copy(bf16[32,256]{1,0:T(8,128)(2,1)} %shard_map.82) | data formatting | bytes 32768

commit v5 on v3

v5 whole, which is shorter than its diff:
```python
import functools
import math

import jax
import jax.numpy as jnp
from jax import lax
from jax.experimental import pallas as pl
from jax.experimental.pallas import tpu as pltpu
from jax.sharding import PartitionSpec as P

MESH = pl.DeviceIdType.MESH
N_DP = 32
PACKED = 80
GROUP = 16
SERVE_Y = (0, 1, 2, 3, 7, 6, 5, 4)
AWAIT_Y = (0, 1, 7, 2, 6, 3, 5, 4)


def flip(bit, other):
    return lax.rem(bit + other, 2)


def group(g):
    return [[y * 4 + half * 2 + g // 2 for half in range(2)] for y in AWAIT_Y[g % 2 * 4:g % 2 * 4 + 4]]


def kernel(
    hidden_hbm, base_hbm, lora_in_hbm, lora_out_hbm, gain_hbm, keys_hbm, values_hbm, lengths_hbm,
    out_ref,
    hidden, base, lora_in, lora_out, gain, keys, values, lengths,
    slots, ups, spread, merged, ordered, turned_keys, bias,
    in_sems, send_dp, send_pair, send_core, recv,
):
    dp, t = lax.axis_index("dp"), lax.axis_index("tensor")
    x, z_lo, core = t // 4, lax.rem(t // 2, 2), lax.rem(t, 2)
    z1, z0 = lax.rem(dp // 2, 2), lax.rem(dp, 2)
    sibling = (dp, x * 4 + z_lo * 2 + (1 - core))
    early, late = z1 == 0, z1 == 1
    early_0, early_1 = jnp.logical_and(early, core == 0), jnp.logical_and(early, core == 1)
    late_0, late_1 = jnp.logical_and(late, core == 0), jnp.logical_and(late, core == 1)
    pair = (dp, x * 4 + (1 - z_lo) * 2 + core)

    def at(y, z_hi, lo, to_core):
        return (y * 4 + z_hi, x * 4 + lo * 2 + to_core)

    def within(half):
        return [at(y, half * 2 + z, z_lo, 0) for z in range(2) for y in SERVE_Y]

    def across(half, to_core):
        return [at(y, half * 2 + z, flip(z_lo, flip(z0, z + 1)), to_core) for z in range(2) for y in SERVE_Y]

    def late_sender(y):
        z = 1 - z_lo
        return at(y, 2 + z, z + z0 - z * z0, 1)

    late_serves = [(at(y, z, 1 - z0, 1), z0 + z - z0 * z == z_lo) for z in range(2) for y in SERVE_Y]
    n_late_serves = jnp.where(z0 == 0, 8, jnp.where(z_lo == 1, 16, 0))

    def load(i):
        src, dst = (
            (lora_in_hbm, lora_in), (lora_out_hbm, lora_out), (hidden_hbm, hidden), (base_hbm, base),
            (keys_hbm, keys), (values_hbm, values), (gain_hbm, gain), (lengths_hbm, lengths),
        )[i]
        return pltpu.make_async_copy(src, dst, in_sems.at[i])

    for i in (0, 1):
        load(i).start()

    barrier = pltpu.get_barrier_semaphore()

    def signal(device):
        pl.semaphore_signal(barrier, inc=1, device_id=device, device_id_type=MESH)

    @pl.when(core == 0)
    def _():
        for device in within(z1):
            @pl.when(device[0] != dp)
            def _():
                signal(device)

    @pl.when(late_0)
    def _():
        for device in across(0, 1):
            signal(device)

    @pl.when(early_1)
    def _():
        for y in AWAIT_Y:
            signal(late_sender(y))
        signal(pair)

    @pl.when(jnp.logical_not(late_0))
    def _():
        signal(sibling)

    @pl.when(early)
    def _():
        for i in range(2, 8):
            load(i).start()

    load(0).wait()
    load(1).wait()
    rows = jnp.transpose(lora_in[...].astype(jnp.float32))
    packed = jnp.concatenate([rows[:PACKED], rows[PACKED:]], axis=1)
    slots[dp] = packed.astype(jnp.bfloat16)
    columns = []
    for lo in range(2):
        even = lora_out[x * 4 + lo * 2].astype(jnp.float32)
        odd = lora_out[x * 4 + lo * 2 + 1].astype(jnp.float32)
        columns.append(jnp.concatenate([even, odd], axis=1))
    ups[dp] = jnp.concatenate(columns, axis=0).astype(jnp.bfloat16)

    def prepare():
        for i in range(4, 8):
            load(i).wait()
        square = (32, 128)
        on_diagonal = lax.broadcasted_iota(jnp.int32, square, 0) == lax.broadcasted_iota(jnp.int32, square, 1)
        length_row = jnp.concatenate([lengths[...], jnp.zeros((1, 96), jnp.int32)], axis=1).astype(jnp.float32)
        length_column = jnp.sum(jnp.where(on_diagonal, length_row, 0.0), axis=1, keepdims=True).astype(jnp.int32)
        tile = (16, 512)
        row = lax.rem(lax.broadcasted_iota(jnp.int32, tile, 0), 8)
        column = lax.broadcasted_iota(jnp.int32, tile, 1)
        own_row = column // 64 == row
        position = lax.rem(column, 64)
        for j in range(4):
            length = jnp.concatenate([length_column[j * 8:j * 8 + 8]] * 2, axis=0)
            bias[j] = jnp.where(jnp.logical_and(own_row, position < length), 0.0, -jnp.inf)
            turned_keys[j] = jnp.transpose(keys[j * 8:j * 8 + 8].reshape(512, 128))
        load(2).wait()
        for g in range(4):
            pieces = [hidden[:, s * 160:s * 160 + 160].astype(jnp.float32) for pair_of in group(g) for s in pair_of]
            ordered[g] = jnp.concatenate(pieces, axis=1).astype(jnp.bfloat16)
        load(3).wait()

    @pl.when(early)
    def _():
        prepare()

    @pl.when(jnp.logical_or(jnp.logical_not(late_1), n_late_serves > 0))
    def _():
        pl.semaphore_wait(barrier, jnp.where(core == 0, 16, jnp.where(early, 18, n_late_serves)))

    def remote(src, dst, send_sem, recv_sem, device):
        return pltpu.make_async_remote_copy(
            src_ref=src, dst_ref=dst, send_sem=send_sem, recv_sem=recv_sem, device_id=device, device_id_type=MESH
        )

    def down(s, send_sem, device):
        return remote(slots.at[s], slots.at[s], send_sem.at[0], recv.at[0, s], device)

    def up(s, send_sem, device):
        return remote(ups.at[s], ups.at[s], send_sem.at[1], recv.at[1, s], device)

    def serve(act):
        @pl.when(late_1)
        def _():
            for i, (device, ours) in enumerate(late_serves):
                @pl.when(ours)
                def _():
                    act(send_dp.at[i], device)

        @pl.when(early_1)
        def _():
            for i, device in enumerate(across(1, 0)):
                act(send_dp.at[i], device)

        @pl.when(core == 0)
        def _():
            for i, device in enumerate(within(z1)):
                @pl.when(device[0] != dp)
                def _():
                    act(send_dp.at[i], device)

    serve(lambda sem, device: up(dp, sem, device).start())
    serve(lambda sem, device: down(dp, sem, device).start())

    @pl.when(late)
    def _():
        for i in range(2, 8):
            load(i).start()

    def half_shards(half):
        return [y * 4 + half * 2 + z for z in range(2) for y in AWAIT_Y]

    def arrive(kind, s):
        kind(s, send_core.at[0], sibling).wait_recv()

    def forward_own(kind, act):
        @pl.when(core == 0)
        def _():
            for i, s in enumerate(half_shards(z1)):
                @pl.when(s != dp)
                def _():
                    act(kind, s, i)

    def forward_other(kind, act, s, i):
        @pl.when(late_0)
        def _():
            act(kind, s, 16 + i)

        @pl.when(early_1)
        def _():
            act(kind, s, i)

            @pl.when(i // 8 != z_lo)
            def _():
                act(kind, s, i, True)

    def pass_on(kind, s, i, to_pair=False):
        if to_pair:
            kind(s, send_pair.at[i % 8], pair).start()
        else:
            arrive(kind, s)
            kind(s, send_core.at[i], sibling).start()

    others = half_shards(1 - z1)
    forward_own(up, pass_on)
    forward_own(down, pass_on)

    @pl.when(late)
    def _():
        prepare()

    for i, s in enumerate(others):
        forward_other(up, pass_on, s, i)

    def from_sibling(kind, s):
        @pl.when(jnp.logical_and(core == 1, s != dp))
        def _():
            arrive(kind, s)

    def others_from_sibling(kind, s):
        @pl.when(jnp.logical_or(early_0, late_1))
        def _():
            arrive(kind, s)

    for s in half_shards(z1):
        from_sibling(up, s)
    for s in others:
        others_from_sibling(up, s)

    lows = ups[...].astype(jnp.float32)
    both = jnp.where(z_lo == 0, lows[:, :8], lows[:, 8:]).reshape(256, 128)
    turned = pltpu.roll(both, 64, 1)
    lane = lax.broadcasted_iota(jnp.int32, (128, 256), 0)
    first = jnp.transpose(jnp.where(core == 0, both, turned))
    second = jnp.transpose(jnp.where(core == 0, turned, both))
    spread[:, :256] = jnp.where(lane < 64, first, 0.0).astype(jnp.bfloat16)
    spread[:, 256:] = jnp.where(lane >= 64, second, 0.0).astype(jnp.bfloat16)

    query = jnp.zeros((32, 256), jnp.float32)
    for g in range(4):
        for k in range(4):
            i = g * 4 + k
            from_sibling(down, half_shards(z1)[i])
            forward_other(down, pass_on, others[i], i)
            others_from_sibling(down, others[i])
        for k, pair_of in enumerate(group(g)):
            for half, s in enumerate(pair_of):
                update = jnp.dot(slots[s], spread[...], preferred_element_type=jnp.float32)
                for part in range(2):
                    base_part = base[s * 160 + part * PACKED:s * 160 + part * PACKED + PACKED].astype(jnp.float32)
                    row = (k * 2 + half) * 160 + part * PACKED
                    merged[g, row:row + PACKED] = (base_part + update[:, part * 256:part * 256 + 256]).astype(jnp.bfloat16)
        query += jnp.dot(ordered[g], merged[g], preferred_element_type=jnp.float32)

    gains = gain[...]
    heads = []
    for h in range(2):
        head = query[:, h * 128:h * 128 + 128]
        inverse = lax.rsqrt(jnp.mean(head * head, axis=-1, keepdims=True) + 1e-06)
        heads.append(head * inverse * gains)
    parts = []
    for j in range(4):
        normed = jnp.concatenate([heads[0][j * 8:j * 8 + 8], heads[1][j * 8:j * 8 + 8]], axis=0).astype(jnp.bfloat16)
        values_tile = values[j * 8:j * 8 + 8].reshape(512, 128)
        scores = jnp.dot(normed, turned_keys[j], preferred_element_type=jnp.float32) / math.sqrt(128) + bias[j]
        expo = jnp.exp(scores - jnp.max(scores, axis=-1, keepdims=True))
        weights = (expo * (1.0 / jnp.sum(expo, axis=-1, keepdims=True))).astype(jnp.bfloat16)
        parts.append(jnp.dot(weights, values_tile, preferred_element_type=jnp.float32))
    out_ref[...] = jnp.concatenate(
        [jnp.concatenate([part[h * 8:h * 8 + 8] for part in parts], axis=0) for h in range(2)], axis=1
    ).astype(jnp.bfloat16)

    serve(lambda sem, device: up(dp, sem, device).wait_send())
    serve(lambda sem, device: down(dp, sem, device).wait_send())

    def sent(kind, s, i, to_pair=False):
        if to_pair:
            kind(s, send_pair.at[i % 8], pair).wait_send()
        else:
            kind(s, send_core.at[i], sibling).wait_send()

    for kind in (up, down):
        forward_own(kind, sent)
        for i, s in enumerate(others):
            forward_other(kind, sent, s, i)


def local(
    hidden, query_base_matrix, input_side_factor, output_side_factor,
    query_norm_gain, cached_key_heads, cached_value_heads, lengths,
):
    bf16 = jnp.bfloat16
    return pl.pallas_call(
        kernel,
        out_shape=jax.ShapeDtypeStruct((32, 256), bf16),
        in_specs=[pl.BlockSpec(memory_space=pl.ANY)] * 8,
        out_specs=pl.BlockSpec(memory_space=pltpu.VMEM),
        scratch_shapes=[
            pltpu.VMEM((32, 5120), bf16),
            pltpu.VMEM((5120, 256), bf16),
            pltpu.VMEM((64, 160), bf16),
            pltpu.VMEM((16, 8, 64), bf16),
            pltpu.VMEM((1, 128), jnp.float32),
            pltpu.VMEM((32, 64, 128), bf16),
            pltpu.VMEM((32, 64, 128), bf16),
            pltpu.VMEM((1, 32), jnp.int32),
            pltpu.VMEM((N_DP, PACKED, 128), bf16),
            pltpu.VMEM((N_DP, GROUP, 128), bf16),
            pltpu.VMEM((128, 512), bf16),
            pltpu.VMEM((4, 1280, 256), bf16),
            pltpu.VMEM((4, 32, 1280), bf16),
            pltpu.VMEM((4, 128, 512), bf16),
            pltpu.VMEM((4, 16, 512), jnp.float32),
            pltpu.SemaphoreType.DMA((8,)),
            pltpu.SemaphoreType.DMA((16, 2)),
            pltpu.SemaphoreType.DMA((8, 2)),
            pltpu.SemaphoreType.DMA((32, 2)),
            pltpu.SemaphoreType.DMA((2, N_DP)),
        ],
        compiler_params=pltpu.CompilerParams(
            collective_id=0, has_side_effects=True, vmem_limit_bytes=56 * 2**20
        ),
        cost_estimate=pl.CostEstimate(flops=260_000_000, bytes_accessed=4_200_000, transcendentals=32768),
    )(
        hidden, query_base_matrix, input_side_factor.T, jnp.transpose(output_side_factor, (1, 2, 0)),
        query_norm_gain.reshape(1, 128), cached_key_heads.reshape(32, 64, 128),
        cached_value_heads.reshape(32, 64, 128), lengths.reshape(1, 32),
    )


def solution(mesh):
    in_specs = (
        P("dp", None),
        P(None, "tensor"),
        P("dp", None),
        P(None, None, "dp"),
        P(),
        P("dp", "tensor", None, None),
        P("dp", "tensor", None, None),
        P("dp"),
    )
    return jax.shard_map(local, mesh=mesh, in_specs=in_specs, out_specs=P("dp", "tensor"), check_vma=False)
```

time: 29.8 us -> 35.7 us (1.20)
  the two profiles are of different devices: /device:TPU:1 before, /device:TPU:196 now
where the time goes in v5:
time: 35.7 us; the launch traced here: 35.5 us
  Pallas kernels  34.1 us (96%)
  local copies, waits for them, and re-layouts  1.32 us (4%)
    pallas_call x1, Pallas kernels, local(): pl.pallas_call(kernel, out_shape=jax.ShapeDtypeStruct((32, 256), bf16), i...  34.1 us
    unnamed x1, local copies, waits for them, and re-layouts  1.32 us

profile of v5, /device:TPU:196, one launch (start us, length us, event | category | flops | bytes accessed | tf_op | source)
XLA Modules:
  0.0 35.5 jit_solution(3931987462593452615)
XLA Ops:
  0.0 34.1 %shard_map.82 = bf16[32,256]{1,0:T(8,128)(2,1)} custom-call(bf16[32,5120]{1,0:T(8,128)(2,1)} %hidden_hbm.1, bf16[5120,256]{1,0:T(8,128)(2,1)} %base_hbm.1, bf16[64,160]{1,0:T(8,128)(2,1)} %bitcast.8, bf16[16,8,64]{2,1,0:T(8,128)(2,1)} %bitcast.9, f32[1,128]{1,0:T(1,128)} %bitcast.10, bf16[32,64,128]{2,1,0:T(8,128)(2,1)} %bitcast.6, ...), custom_call_target="tpu_custom_call" | custom-call | flops 260000000 | bytes 4200000 | tf_op jit(solution)/shard_map/pallas_call | solution.py:305
  34.1 1.3 %copy.10 = bf16[32,256]{1,0:T(8,128)(2,1)} copy(bf16[32,256]{1,0:T(8,128)(2,1)} %shard_map.82) | data formatting | bytes 32768

commit v6 on v5

--- a/solution.py
+++ b/solution.py
@@ -20,15 +20,15 @@
     return lax.rem(bit + other, 2)
 
 
-def group(g):
-    return [[y * 4 + half * 2 + g // 2 for half in range(2)] for y in AWAIT_Y[g % 2 * 4:g % 2 * 4 + 4]]
+def chunk(half, z):
+    return [y * 4 + half * 2 + z for y in AWAIT_Y]
 
 
 def kernel(
     hidden_hbm, base_hbm, lora_in_hbm, lora_out_hbm, gain_hbm, keys_hbm, values_hbm, lengths_hbm,
     out_ref,
     hidden, base, lora_in, lora_out, gain, keys, values, lengths,
-    slots, ups, spread, merged, ordered, turned_keys, bias,
+    slots, ups, own_ups, spread, merged, ordered, turned_keys, bias,
     in_sems, send_dp, send_pair, send_core, recv,
 ):
     dp, t = lax.axis_index("dp"), lax.axis_index("tensor")
@@ -38,7 +38,9 @@
     early, late = z1 == 0, z1 == 1
     early_0, early_1 = jnp.logical_and(early, core == 0), jnp.logical_and(early, core == 1)
     late_0, late_1 = jnp.logical_and(late, core == 0), jnp.logical_and(late, core == 1)
-    pair = (dp, x * 4 + (1 - z_lo) * 2 + core)
+    takes = 1 - flip(x // 2, lax.rem(x, 2))
+    pair = (dp, (x + 1 - 2 * lax.rem(x, 2)) * 4 + z_lo * 2 + core)
+    crosses = jnp.logical_and(core == 1, z0 == takes)
 
     def at(y, z_hi, lo, to_core):
         return (y * 4 + z_hi, x * 4 + lo * 2 + to_core)
@@ -49,12 +51,8 @@
     def across(half, to_core):
         return [at(y, half * 2 + z, flip(z_lo, flip(z0, z + 1)), to_core) for z in range(2) for y in SERVE_Y]
 
-    def late_sender(y):
-        z = 1 - z_lo
-        return at(y, 2 + z, z + z0 - z * z0, 1)
-
-    late_serves = [(at(y, z, 1 - z0, 1), z0 + z - z0 * z == z_lo) for z in range(2) for y in SERVE_Y]
-    n_late_serves = jnp.where(z0 == 0, 8, jnp.where(z_lo == 1, 16, 0))
+    def crossing_to_here(half, from_core):
+        return [at(y, half * 2 + takes, flip(z_lo, flip(z0, takes + 1)), from_core) for y in SERVE_Y]
 
     def load(i):
         src, dst = (
@@ -80,13 +78,14 @@
 
     @pl.when(late_0)
     def _():
-        for device in across(0, 1):
+        for device in crossing_to_here(0, 1):
             signal(device)
+        signal(pair)
 
     @pl.when(early_1)
     def _():
-        for y in AWAIT_Y:
-            signal(late_sender(y))
+        for device in crossing_to_here(1, 1):
+            signal(device)
         signal(pair)
 
     @pl.when(jnp.logical_not(late_0))
@@ -103,12 +102,15 @@
     rows = jnp.transpose(lora_in[...].astype(jnp.float32))
     packed = jnp.concatenate([rows[:PACKED], rows[PACKED:]], axis=1)
     slots[dp] = packed.astype(jnp.bfloat16)
-    columns = []
+    x_pair = x // 2 * 2
     for lo in range(2):
-        even = lora_out[x * 4 + lo * 2].astype(jnp.float32)
-        odd = lora_out[x * 4 + lo * 2 + 1].astype(jnp.float32)
-        columns.append(jnp.concatenate([even, odd], axis=1))
-    ups[dp] = jnp.concatenate(columns, axis=0).astype(jnp.bfloat16)
+        columns = []
+        for k in range(2):
+            even = lora_out[(x_pair + k) * 4 + lo * 2].astype(jnp.float32)
+            odd = lora_out[(x_pair + k) * 4 + lo * 2 + 1].astype(jnp.float32)
+            columns.append(jnp.concatenate([even, odd], axis=1))
+        own_ups[lo] = jnp.concatenate(columns, axis=0).astype(jnp.bfloat16)
+    ups[dp] = own_ups[z_lo]
 
     def prepare():
         for i in range(4, 8):
@@ -127,18 +129,18 @@
             bias[j] = jnp.where(jnp.logical_and(own_row, position < length), 0.0, -jnp.inf)
             turned_keys[j] = jnp.transpose(keys[j * 8:j * 8 + 8].reshape(512, 128))
         load(2).wait()
-        for g in range(4):
-            pieces = [hidden[:, s * 160:s * 160 + 160].astype(jnp.float32) for pair_of in group(g) for s in pair_of]
-            ordered[g] = jnp.concatenate(pieces, axis=1).astype(jnp.bfloat16)
+        for c in range(4):
+            pieces = [hidden[:, s * 160:s * 160 + 160].astype(jnp.float32) for s in chunk(c // 2, c % 2)]
+            ordered[c] = jnp.concatenate(pieces, axis=1).astype(jnp.bfloat16)
         load(3).wait()
 
     @pl.when(early)
     def _():
         prepare()
 
-    @pl.when(jnp.logical_or(jnp.logical_not(late_1), n_late_serves > 0))
-    def _():
-        pl.semaphore_wait(barrier, jnp.where(core == 0, 16, jnp.where(early, 18, n_late_serves)))
+    @pl.when(jnp.logical_or(jnp.logical_not(late_1), crosses))
+    def _():
+        pl.semaphore_wait(barrier, jnp.where(early_1, jnp.where(crosses, 18, 2), jnp.where(late_0, 17, 16)))
 
     def remote(src, dst, send_sem, recv_sem, device):
         return pltpu.make_async_remote_copy(
@@ -151,15 +153,20 @@
     def up(s, send_sem, device):
         return remote(ups.at[s], ups.at[s], send_sem.at[1], recv.at[1, s], device)
 
+    def own_up(send_sem, device):
+        z_lo_there = lax.rem(device[1] // 2, 2)
+        return remote(own_ups.at[z_lo_there], ups.at[dp], send_sem.at[1], recv.at[1, dp], device)
+
+    def own_down(send_sem, device):
+        return down(dp, send_sem, device)
+
     def serve(act):
-        @pl.when(late_1)
-        def _():
-            for i, (device, ours) in enumerate(late_serves):
-                @pl.when(ours)
-                def _():
-                    act(send_dp.at[i], device)
-
-        @pl.when(early_1)
+        @pl.when(jnp.logical_and(late, crosses))
+        def _():
+            for i, device in enumerate(across(0, 1)):
+                act(send_dp.at[i], device)
+
+        @pl.when(jnp.logical_and(early, crosses))
         def _():
             for i, device in enumerate(across(1, 0)):
                 act(send_dp.at[i], device)
@@ -171,8 +178,8 @@
                 def _():
                     act(send_dp.at[i], device)
 
-    serve(lambda sem, device: up(dp, sem, device).start())
-    serve(lambda sem, device: down(dp, sem, device).start())
+    serve(lambda sem, device: own_up(sem, device).start())
+    serve(lambda sem, device: own_down(sem, device).start())
 
     @pl.when(late)
     def _():
@@ -180,7 +187,7 @@
             load(i).start()
 
     def half_shards(half):
-        return [y * 4 + half * 2 + z for z in range(2) for y in AWAIT_Y]
+        return chunk(half, 0) + chunk(half, 1)
 
     def arrive(kind, s):
         kind(s, send_core.at[0], sibling).wait_recv()
@@ -202,9 +209,9 @@
         def _():
             act(kind, s, i)
 
-            @pl.when(i // 8 != z_lo)
-            def _():
-                act(kind, s, i, True)
+        @pl.when(jnp.logical_and(jnp.logical_or(late_0, early_1), i // 8 == takes))
+        def _():
+            act(kind, s, i, True)
 
     def pass_on(kind, s, i, to_pair=False):
         if to_pair:
@@ -221,26 +228,35 @@
     def _():
         prepare()
 
-    for i, s in enumerate(others):
-        forward_other(up, pass_on, s, i)
-
-    def from_sibling(kind, s):
-        @pl.when(jnp.logical_and(core == 1, s != dp))
-        def _():
-            arrive(kind, s)
-
-    def others_from_sibling(kind, s):
+    def forward_others(kind, places):
+        for i in places:
+            forward_other(kind, pass_on, others[i], i)
+
+    def own_from_sibling(kind):
+        @pl.when(core == 1)
+        def _():
+            for s in half_shards(z1):
+                @pl.when(s != dp)
+                def _():
+                    arrive(kind, s)
+
+    def others_from_sibling(kind, places):
         @pl.when(jnp.logical_or(early_0, late_1))
         def _():
-            arrive(kind, s)
-
-    for s in half_shards(z1):
-        from_sibling(up, s)
-    for s in others:
-        others_from_sibling(up, s)
+            for i in places:
+                arrive(kind, others[i])
+
+    z_0, z_1 = range(8), range(8, 16)
+    forward_others(up, z_0)
+    forward_others(down, z_0)
+    forward_others(up, z_1)
+    own_from_sibling(up)
+    own_from_sibling(down)
+    others_from_sibling(up, z_0)
+    others_from_sibling(up, z_1)
 
     lows = ups[...].astype(jnp.float32)
-    both = jnp.where(z_lo == 0, lows[:, :8], lows[:, 8:]).reshape(256, 128)
+    both = jnp.where(lax.rem(x, 2) == 0, lows[:, :8], lows[:, 8:]).reshape(256, 128)
     turned = pltpu.roll(both, 64, 1)
     lane = lax.broadcasted_iota(jnp.int32, (128, 256), 0)
     first = jnp.transpose(jnp.where(core == 0, both, turned))
@@ -248,21 +264,22 @@
     spread[:, :256] = jnp.where(lane < 64, first, 0.0).astype(jnp.bfloat16)
     spread[:, 256:] = jnp.where(lane >= 64, second, 0.0).astype(jnp.bfloat16)
 
-    query = jnp.zeros((32, 256), jnp.float32)
-    for g in range(4):
-        for k in range(4):
-            i = g * 4 + k
-            from_sibling(down, half_shards(z1)[i])
-            forward_other(down, pass_on, others[i], i)
-            others_from_sibling(down, others[i])
-        for k, pair_of in enumerate(group(g)):
-            for half, s in enumerate(pair_of):
-                update = jnp.dot(slots[s], spread[...], preferred_element_type=jnp.float32)
-                for part in range(2):
-                    base_part = base[s * 160 + part * PACKED:s * 160 + part * PACKED + PACKED].astype(jnp.float32)
-                    row = (k * 2 + half) * 160 + part * PACKED
-                    merged[g, row:row + PACKED] = (base_part + update[:, part * 256:part * 256 + 256]).astype(jnp.bfloat16)
-        query += jnp.dot(ordered[g], merged[g], preferred_element_type=jnp.float32)
+    def project(half, z):
+        at = half * 2 + z
+        for k, s in enumerate(chunk(half, z)):
+            update = jnp.dot(slots[s], spread[...], preferred_element_type=jnp.float32)
+            for part in range(2):
+                rows = pl.ds(pl.multiple_of(s * 160 + part * PACKED, 16), PACKED)
+                total = base[rows, :].astype(jnp.float32) + update[:, part * 256:part * 256 + 256]
+                merged[at, k * 160 + part * PACKED:k * 160 + part * PACKED + PACKED] = total.astype(jnp.bfloat16)
+        return jnp.dot(ordered[at], merged[at], preferred_element_type=jnp.float32)
+
+    query = project(z1, 0) + project(z1, 1)
+    forward_others(down, z_1)
+    others_from_sibling(down, z_0)
+    query += project(1 - z1, 0)
+    others_from_sibling(down, z_1)
+    query += project(1 - z1, 1)
 
     gains = gain[...]
     heads = []
@@ -282,8 +299,8 @@
         [jnp.concatenate([part[h * 8:h * 8 + 8] for part in parts], axis=0) for h in range(2)], axis=1
     ).astype(jnp.bfloat16)
 
-    serve(lambda sem, device: up(dp, sem, device).wait_send())
-    serve(lambda sem, device: down(dp, sem, device).wait_send())
+    serve(lambda sem, device: own_up(sem, device).wait_send())
+    serve(lambda sem, device: own_down(sem, device).wait_send())
 
     def sent(kind, s, i, to_pair=False):
         if to_pair:
@@ -318,6 +335,7 @@
             pltpu.VMEM((1, 32), jnp.int32),
             pltpu.VMEM((N_DP, PACKED, 128), bf16),
             pltpu.VMEM((N_DP, GROUP, 128), bf16),
+            pltpu.VMEM((2, GROUP, 128), bf16),
             pltpu.VMEM((128, 512), bf16),
             pltpu.VMEM((4, 1280, 256), bf16),
             pltpu.VMEM((4, 32, 1280), bf16),

time: 35.7 us -> 36.1 us (1.011)
  the two profiles are of different devices: /device:TPU:196 before, /device:TPU:325 now
where the time goes in v6:
time: 36.1 us; the launch traced here: 35.9 us
  Pallas kernels  34.6 us (96%)
  local copies, waits for them, and re-layouts  1.32 us (4%)
    pallas_call x1, Pallas kernels, local(): pl.pallas_call(kernel, out_shape=jax.ShapeDtypeStruct((32, 256), bf16), i...  34.6 us
    unnamed x1, local copies, waits for them, and re-layouts  1.32 us

profile of v6, /device:TPU:325, one launch (start us, length us, event | category | flops | bytes accessed | tf_op | source)
XLA Modules:
  0.0 35.9 jit_solution(15594166348991019544)
XLA Ops:
  0.0 34.6 %shard_map.82 = bf16[32,256]{1,0:T(8,128)(2,1)} custom-call(bf16[32,5120]{1,0:T(8,128)(2,1)} %hidden_hbm.1, bf16[5120,256]{1,0:T(8,128)(2,1)} %base_hbm.1, bf16[64,160]{1,0:T(8,128)(2,1)} %bitcast.8, bf16[16,8,64]{2,1,0:T(8,128)(2,1)} %bitcast.9, f32[1,128]{1,0:T(1,128)} %bitcast.10, bf16[32,64,128]{2,1,0:T(8,128)(2,1)} %bitcast.6, ...), custom_call_target="tpu_custom_call" | custom-call | flops 260000000 | bytes 4200000 | tf_op jit(solution)/shard_map/pallas_call | solution.py:322
  34.6 1.3 %copy.10 = bf16[32,256]{1,0:T(8,128)(2,1)} copy(bf16[32,256]{1,0:T(8,128)(2,1)} %shard_map.82) | data formatting | bytes 32768

commit v7 on v6

--- a/solution.py
+++ b/solution.py
@@ -29,7 +29,7 @@
     out_ref,
     hidden, base, lora_in, lora_out, gain, keys, values, lengths,
     slots, ups, own_ups, spread, merged, ordered, turned_keys, bias,
-    in_sems, send_dp, send_pair, send_core, recv,
+    in_sems, send_dp, send_pair, send_core, recv, recv_core,
 ):
     dp, t = lax.axis_index("dp"), lax.axis_index("tensor")
     x, z_lo, core = t // 4, lax.rem(t // 2, 2), lax.rem(t, 2)
@@ -78,9 +78,8 @@
 
     @pl.when(late_0)
     def _():
-        for device in crossing_to_here(0, 1):
+        for device in across(0, 1):
             signal(device)
-        signal(pair)
 
     @pl.when(early_1)
     def _():
@@ -140,46 +139,50 @@
 
     @pl.when(jnp.logical_or(jnp.logical_not(late_1), crosses))
     def _():
-        pl.semaphore_wait(barrier, jnp.where(early_1, jnp.where(crosses, 18, 2), jnp.where(late_0, 17, 16)))
+        pl.semaphore_wait(barrier, jnp.where(early_1, 18, 16))
 
     def remote(src, dst, send_sem, recv_sem, device):
         return pltpu.make_async_remote_copy(
             src_ref=src, dst_ref=dst, send_sem=send_sem, recv_sem=recv_sem, device_id=device, device_id_type=MESH
         )
 
-    def down(s, send_sem, device):
-        return remote(slots.at[s], slots.at[s], send_sem.at[0], recv.at[0, s], device)
-
-    def up(s, send_sem, device):
-        return remote(ups.at[s], ups.at[s], send_sem.at[1], recv.at[1, s], device)
-
-    def own_up(send_sem, device):
+    def down(s, send_sem, recv_sem, device):
+        return remote(slots.at[s], slots.at[s], send_sem.at[0], recv_sem.at[0], device)
+
+    def up(s, send_sem, recv_sem, device):
+        return remote(ups.at[s], ups.at[s], send_sem.at[1], recv_sem.at[1], device)
+
+    def own_up(device):
         z_lo_there = lax.rem(device[1] // 2, 2)
-        return remote(own_ups.at[z_lo_there], ups.at[dp], send_sem.at[1], recv.at[1, dp], device)
-
-    def own_down(send_sem, device):
-        return down(dp, send_sem, device)
+        return remote(own_ups.at[z_lo_there], ups.at[dp], send_dp.at[1], recv.at[dp, 1], device)
+
+    def own_down(device):
+        return down(dp, send_dp, recv.at[dp], device)
+
+    def many(kind, n, send_sem, recv_sem):
+        ref, at = (slots, 0) if kind is down else (ups, 1)
+        return remote(ref.at[pl.ds(0, n)], ref.at[pl.ds(0, n)], send_sem.at[at], recv_sem.at[at], sibling)
 
     def serve(act):
         @pl.when(jnp.logical_and(late, crosses))
         def _():
-            for i, device in enumerate(across(0, 1)):
-                act(send_dp.at[i], device)
-
-        @pl.when(jnp.logical_and(early, crosses))
-        def _():
-            for i, device in enumerate(across(1, 0)):
-                act(send_dp.at[i], device)
+            for device in across(0, 1):
+                act(device)
+
+        @pl.when(early_1)
+        def _():
+            for device in across(1, 0):
+                act(device)
 
         @pl.when(core == 0)
         def _():
-            for i, device in enumerate(within(z1)):
+            for device in within(z1):
                 @pl.when(device[0] != dp)
                 def _():
-                    act(send_dp.at[i], device)
-
-    serve(lambda sem, device: own_up(sem, device).start())
-    serve(lambda sem, device: own_down(sem, device).start())
+                    act(device)
+
+    serve(lambda device: own_up(device).start())
+    serve(lambda device: own_down(device).start())
 
     @pl.when(late)
     def _():
@@ -189,71 +192,58 @@
     def half_shards(half):
         return chunk(half, 0) + chunk(half, 1)
 
-    def arrive(kind, s):
-        kind(s, send_core.at[0], sibling).wait_recv()
-
-    def forward_own(kind, act):
+    def pass_on(kind, s, group):
+        kind(s, send_core, recv.at[s], sibling).wait_recv()
+        kind(s, send_core, recv_core.at[group], sibling).start()
+
+    def pass_own(kind):
         @pl.when(core == 0)
-        def _():
-            for i, s in enumerate(half_shards(z1)):
-                @pl.when(s != dp)
-                def _():
-                    act(kind, s, i)
-
-    def forward_other(kind, act, s, i):
-        @pl.when(late_0)
-        def _():
-            act(kind, s, 16 + i)
-
-        @pl.when(early_1)
-        def _():
-            act(kind, s, i)
-
-        @pl.when(jnp.logical_and(jnp.logical_or(late_0, early_1), i // 8 == takes))
-        def _():
-            act(kind, s, i, True)
-
-    def pass_on(kind, s, i, to_pair=False):
-        if to_pair:
-            kind(s, send_pair.at[i % 8], pair).start()
-        else:
-            arrive(kind, s)
-            kind(s, send_core.at[i], sibling).start()
-
-    others = half_shards(1 - z1)
-    forward_own(up, pass_on)
-    forward_own(down, pass_on)
-
-    @pl.when(late)
-    def _():
-        prepare()
-
-    def forward_others(kind, places):
-        for i in places:
-            forward_other(kind, pass_on, others[i], i)
-
-    def own_from_sibling(kind):
-        @pl.when(core == 1)
         def _():
             for s in half_shards(z1):
                 @pl.when(s != dp)
                 def _():
-                    arrive(kind, s)
-
-    def others_from_sibling(kind, places):
-        @pl.when(jnp.logical_or(early_0, late_1))
-        def _():
-            for i in places:
-                arrive(kind, others[i])
-
-    z_0, z_1 = range(8), range(8, 16)
-    forward_others(up, z_0)
-    forward_others(down, z_0)
-    forward_others(up, z_1)
-    own_from_sibling(up)
-    own_from_sibling(down)
-    others_from_sibling(up, z_0)
-    others_from_sibling(up, z_1)
+                    pass_on(kind, s, 0)
+
+    others = chunk(1 - z1, takes) + chunk(1 - z1, 1 - takes)
+
+    def pass_straight(kind, role):
+        @pl.when(role)
+        def _():
+            for s in others[:8]:
+                pass_on(kind, s, 1)
+
+                @pl.when(early)
+                def _():
+                    kind(s, send_pair, recv.at[s], pair).start()
+
+    def pass_rest(kind):
+        @pl.when(jnp.logical_or(late_0, early_1))
+        def _():
+            for i, s in enumerate(others[8:]):
+                pass_on(kind, s, 2 + i // 4)
+
+    def from_sibling(kind, group):
+        role = core == 1 if group == 0 else jnp.logical_or(early_0, late_1)
+
+        @pl.when(role)
+        def _():
+            many(kind, (15, 8, 4, 4)[group], send_core, recv_core.at[group]).wait_recv()
+
+    pass_own(up)
+    pass_own(down)
+
+    @pl.when(late)
+    def _():
+        prepare()
+
+    pass_straight(up, jnp.logical_or(late_0, early_1))
+    pass_straight(down, early_1)
+    pass_rest(up)
+    from_sibling(up, 0)
+    from_sibling(down, 0)
+    from_sibling(up, 1)
+    from_sibling(up, 2)
+    from_sibling(up, 3)
 
     lows = ups[...].astype(jnp.float32)
     both = jnp.where(lax.rem(x, 2) == 0, lows[:, :8], lows[:, 8:]).reshape(256, 128)
@@ -264,22 +254,29 @@
     spread[:, :256] = jnp.where(lane < 64, first, 0.0).astype(jnp.bfloat16)
     spread[:, 256:] = jnp.where(lane >= 64, second, 0.0).astype(jnp.bfloat16)
 
-    def project(half, z):
+    def project(half, z, places=(0, 8)):
         at = half * 2 + z
+        begin, end = places
         for k, s in enumerate(chunk(half, z)):
+            if not begin <= k < end:
+                continue
             update = jnp.dot(slots[s], spread[...], preferred_element_type=jnp.float32)
             for part in range(2):
                 rows = pl.ds(pl.multiple_of(s * 160 + part * PACKED, 16), PACKED)
                 total = base[rows, :].astype(jnp.float32) + update[:, part * 256:part * 256 + 256]
                 merged[at, k * 160 + part * PACKED:k * 160 + part * PACKED + PACKED] = total.astype(jnp.bfloat16)
-        return jnp.dot(ordered[at], merged[at], preferred_element_type=jnp.float32)
+        columns = slice(begin * 160, end * 160)
+        return jnp.dot(ordered[at, :, columns], merged[at, columns], preferred_element_type=jnp.float32)
 
     query = project(z1, 0) + project(z1, 1)
-    forward_others(down, z_1)
-    others_from_sibling(down, z_0)
-    query += project(1 - z1, 0)
-    others_from_sibling(down, z_1)
-    query += project(1 - z1, 1)
+    pass_straight(down, late_0)
+    pass_rest(down)
+    from_sibling(down, 1)
+    query += project(1 - z1, takes)
+    from_sibling(down, 2)
+    query += project(1 - z1, 1 - takes, (0, 4))
+    from_sibling(down, 3)
+    query += project(1 - z1, 1 - takes, (4, 8))
 
     gains = gain[...]
     heads = []
@@ -291,7 +288,7 @@
     for j in range(4):
         normed = jnp.concatenate([heads[0][j * 8:j * 8 + 8], heads[1][j * 8:j * 8 + 8]], axis=0).astype(jnp.bfloat16)
         values_tile = values[j * 8:j * 8 + 8].reshape(512, 128)
-        scores = jnp.dot(normed, turned_keys[j], preferred_element_type=jnp.float32) / math.sqrt(128) + bias[j]
+        scores = jnp.dot(normed, turned_keys[j], preferred_element_type=jnp.float32) * (1.0 / math.sqrt(128)) + bias[j]
         expo = jnp.exp(scores - jnp.max(scores, axis=-1, keepdims=True))
         weights = (expo * (1.0 / jnp.sum(expo, axis=-1, keepdims=True))).astype(jnp.bfloat16)
         parts.append(jnp.dot(weights, values_tile, preferred_element_type=jnp.float32))
@@ -299,19 +296,31 @@
         [jnp.concatenate([part[h * 8:h * 8 + 8] for part in parts], axis=0) for h in range(2)], axis=1
     ).astype(jnp.bfloat16)
 
-    serve(lambda sem, device: own_up(sem, device).wait_send())
-    serve(lambda sem, device: own_down(sem, device).wait_send())
-
-    def sent(kind, s, i, to_pair=False):
-        if to_pair:
-            kind(s, send_pair.at[i % 8], pair).wait_send()
-        else:
-            kind(s, send_core.at[i], sibling).wait_send()
-
-    for kind in (up, down):
-        forward_own(kind, sent)
-        for i, s in enumerate(others):
-            forward_other(kind, sent, s, i)
+    def sent(n, sem):
+        for kind in (up, down):
+            many(kind, n, sem, recv_core.at[0]).wait_send()
+
+    @pl.when(core == 0)
+    def _():
+        sent(15, send_dp)
+
+    @pl.when(early_0)
+    def _():
+        sent(15, send_core)
+
+    @pl.when(late_0)
+    def _():
+        sent(31, send_core)
+
+    @pl.when(early_1)
+    def _():
+        sent(16, send_dp)
+        sent(16, send_core)
+        sent(8, send_pair)
+
+    @pl.when(jnp.logical_and(late, crosses))
+    def _():
+        sent(16, send_dp)
 
 
 def local(
@@ -322,7 +331,7 @@
     return pl.pallas_call(
         kernel,
         out_shape=jax.ShapeDtypeStruct((32, 256), bf16),
-        in_specs=[pl.BlockSpec(memory_space=pl.ANY)] * 8,
+        in_specs=[pl.BlockSpec(memory_space=pltpu.HBM)] * 8,
         out_specs=pl.BlockSpec(memory_space=pltpu.VMEM),
         scratch_shapes=[
             pltpu.VMEM((32, 5120), bf16),
@@ -342,10 +351,11 @@
             pltpu.VMEM((4, 128, 512), bf16),
             pltpu.VMEM((4, 16, 512), jnp.float32),
             pltpu.SemaphoreType.DMA((8,)),
-            pltpu.SemaphoreType.DMA((16, 2)),
-            pltpu.SemaphoreType.DMA((8, 2)),
-            pltpu.SemaphoreType.DMA((32, 2)),
-            pltpu.SemaphoreType.DMA((2, N_DP)),
+            pltpu.SemaphoreType.DMA((2,)),
+            pltpu.SemaphoreType.DMA((2,)),
+            pltpu.SemaphoreType.DMA((2,)),
+            pltpu.SemaphoreType.DMA((N_DP, 2)),
+            pltpu.SemaphoreType.DMA((4, 2)),
         ],
         compiler_params=pltpu.CompilerParams(
             collective_id=0, has_side_effects=True, vmem_limit_bytes=56 * 2**20

time: 36.1 us -> 28.3 us (0.78)
  the two profiles are of different devices: /device:TPU:325 before, /device:TPU:1 now
where the time goes in v7:
time: 28.3 us; the launch traced here: 27.9 us
  Pallas kernels  26.6 us (94%)
  local copies, waits for them, and re-layouts  1.32 us (5%)
    pallas_call x1, Pallas kernels, local(): pl.pallas_call(kernel, out_shape=jax.ShapeDtypeStruct((32, 256), bf16), i...  26.6 us
    unnamed x1, local copies, waits for them, and re-layouts  1.32 us

profile of v7, /device:TPU:1, one launch (start us, length us, event | category | flops | bytes accessed | tf_op | source)
XLA Modules:
  0.0 27.9 jit_solution(5972996510084074882)
XLA Ops:
  0.0 26.6 %shard_map.82 = bf16[32,256]{1,0:T(8,128)(2,1)} custom-call(bf16[32,5120]{1,0:T(8,128)(2,1)} %hidden_hbm.1, bf16[5120,256]{1,0:T(8,128)(2,1)} %base_hbm.1, bf16[64,160]{1,0:T(8,128)(2,1)} %bitcast.8, bf16[16,8,64]{2,1,0:T(8,128)(2,1)} %bitcast.9, f32[1,128]{1,0:T(1,128)} %bitcast.10, bf16[32,64,128]{2,1,0:T(8,128)(2,1)} %bitcast.6, ...), custom_call_target="tpu_custom_call" | custom-call | flops 260000000 | bytes 4200000 | tf_op jit(solution)/shard_map/pallas_call | solution.py:331
  26.6 1.3 %copy.10 = bf16[32,256]{1,0:T(8,128)(2,1)} copy(bf16[32,256]{1,0:T(8,128)(2,1)} %shard_map.82) | data formatting | bytes 32768

commit v8 on v7

--- a/solution.py
+++ b/solution.py
@@ -51,6 +51,9 @@
     def across(half, to_core):
         return [at(y, half * 2 + z, flip(z_lo, flip(z0, z + 1)), to_core) for z in range(2) for y in SERVE_Y]
 
+    to_late = [at(y, 2 + z_lo, lo, 0) for lo in range(2) for y in SERVE_Y]
+    from_early = [at(y, z, z0, 1) for z in range(2) for y in SERVE_Y]
+
     def crossing_to_here(half, from_core):
         return [at(y, half * 2 + takes, flip(z_lo, flip(z0, takes + 1)), from_core) for y in SERVE_Y]
 
@@ -69,6 +72,11 @@
     def signal(device):
         pl.semaphore_signal(barrier, inc=1, device_id=device, device_id_type=MESH)
 
+    @pl.when(late_0)
+    def _():
+        for device in from_early:
+            signal(device)
+
     @pl.when(core == 0)
     def _():
         for device in within(z1):
@@ -76,11 +84,6 @@
             def _():
                 signal(device)
 
-    @pl.when(late_0)
-    def _():
-        for device in across(0, 1):
-            signal(device)
-
     @pl.when(early_1)
     def _():
         for device in crossing_to_here(1, 1):
@@ -96,11 +99,7 @@
         for i in range(2, 8):
             load(i).start()
 
-    load(0).wait()
     load(1).wait()
-    rows = jnp.transpose(lora_in[...].astype(jnp.float32))
-    packed = jnp.concatenate([rows[:PACKED], rows[PACKED:]], axis=1)
-    slots[dp] = packed.astype(jnp.bfloat16)
     x_pair = x // 2 * 2
     for lo in range(2):
         columns = []
@@ -171,7 +170,7 @@
 
         @pl.when(early_1)
         def _():
-            for device in across(1, 0):
+            for device in to_late:
                 act(device)
 
         @pl.when(core == 0)
@@ -182,6 +181,12 @@
                     act(device)
 
     serve(lambda device: own_up(device).start())
+
+    load(0).wait()
+    rows = jnp.transpose(lora_in[...].astype(jnp.float32))
+    packed = jnp.concatenate([rows[:PACKED], rows[PACKED:]], axis=1)
+    slots[dp] = packed.astype(jnp.bfloat16)
+
     serve(lambda device: own_down(device).start())
 
     @pl.when(late)
@@ -216,11 +221,12 @@
                 def _():
                     kind(s, send_pair, recv.at[s], pair).start()
 
-    def pass_rest(kind):
+    def pass_rest(kind, groups=(2, 3)):
         @pl.when(jnp.logical_or(late_0, early_1))
         def _():
-            for i, s in enumerate(others[8:]):
-                pass_on(kind, s, 2 + i // 4)
+            for group in groups:
+                for s in others[group * 4:group * 4 + 4]:
+                    pass_on(kind, s, group)
 
     def from_sibling(kind, group):
         role = core == 1 if group == 0 else jnp.logical_or(early_0, late_1)
@@ -270,11 +276,12 @@
 
     query = project(z1, 0) + project(z1, 1)
     pass_straight(down, late_0)
-    pass_rest(down)
     from_sibling(down, 1)
     query += project(1 - z1, takes)
+    pass_rest(down, (2,))
     from_sibling(down, 2)
     query += project(1 - z1, 1 - takes, (0, 4))
+    pass_rest(down, (3,))
     from_sibling(down, 3)
     query += project(1 - z1, 1 - takes, (4, 8))
 
@@ -358,7 +365,7 @@
             pltpu.SemaphoreType.DMA((4, 2)),
         ],
         compiler_params=pltpu.CompilerParams(
-            collective_id=0, has_side_effects=True, vmem_limit_bytes=56 * 2**20
+            collective_id=0, has_side_effects=True, vmem_limit_bytes=54 * 2**20 - 100_000
         ),
         cost_estimate=pl.CostEstimate(flops=260_000_000, bytes_accessed=4_200_000, transcendentals=32768),
     )(

time: 28.3 us -> 29.5 us (1.042)
  the two profiles are of different devices: /device:TPU:1 before, /device:TPU:132 now
where the time goes in v8:
time: 29.5 us; the launch traced here: 29.3 us
  Pallas kernels  27.4 us (93%)
  local copies, waits for them, and re-layouts  1.92 us (7%)
    pallas_call x1, Pallas kernels, local(): pl.pallas_call(kernel, out_shape=jax.ShapeDtypeStruct((32, 256), bf16), i...  27.4 us
    unnamed x5, local copies, waits for them, and re-layouts  1.92 us

profile of v8, /device:TPU:132, one launch (start us, length us, event | category | flops | bytes accessed | tf_op | source)
XLA Modules:
  0.0 29.3 jit_solution(10500196391709434001)
XLA Ops:
  0.0 0.0 copy-start
  0.0 0.7 %copy-done = f32[128]{0:T(128)S(1)} copy-done((f32[128]{0:T(128)S(1)}, f32[128]{0:T(128)}, u32[]{:S(2)}) %copy-start) | copy-done | bytes 536
  0.7 0.0 copy-start.1
  0.7 0.7 %copy-done.1 = s32[32]{0:T(128)S(1)} copy-done((s32[32]{0:T(128)S(1)}, s32[32]{0:T(128)}, u32[]{:S(2)}) %copy-start.1) | copy-done | bytes 152
  1.3 27.4 %shard_map.82 = bf16[32,256]{1,0:T(8,128)(2,1)S(1)} custom-call(bf16[32,5120]{1,0:T(8,128)(2,1)} %hidden_hbm.1, bf16[5120,256]{1,0:T(8,128)(2,1)} %base_hbm.1, bf16[64,160]{1,0:T(8,128)(2,1)} %bitcast.10, bf16[16,8,64]{2,1,0:T(8,128)(2,1)} %bitcast.11, f32[1,128]{1,0:T(1,128)S(1)} %bitcast.6, bf16[32,64,128]{2,1,0:T(8,128)(2,1)} %bitcast.8, ...), custom_call_target="tpu_custom_call" | custom-call | flops 260000000 | bytes 4200000 | tf_op jit(solution)/shard_map/pallas_call | solution.py:338
  28.7 0.6 %copy.10 = bf16[32,256]{1,0:T(8,128)(2,1)} copy(bf16[32,256]{1,0:T(8,128)(2,1)S(1)} %shard_map.82) | data formatting | bytes 32768
Async XLA Ops:
  0.0 0.7 %copy-start = (f32[128]{0:T(128)S(1)}, f32[128]{0:T(128)}, u32[]{:S(2)}) copy-start(f32[128]{0:T(128)} %param.12) | copy-start | bytes 1540
  0.7 0.7 %copy-start.1 = (s32[32]{0:T(128)S(1)}, s32[32]{0:T(128)}, u32[]{:S(2)}) copy-start(s32[32]{0:T(128)} %param.15) | copy-start | bytes 388

commit v9 on v8

--- a/solution.py
+++ b/solution.py
@@ -51,9 +51,6 @@
     def across(half, to_core):
         return [at(y, half * 2 + z, flip(z_lo, flip(z0, z + 1)), to_core) for z in range(2) for y in SERVE_Y]
 
-    to_late = [at(y, 2 + z_lo, lo, 0) for lo in range(2) for y in SERVE_Y]
-    from_early = [at(y, z, z0, 1) for z in range(2) for y in SERVE_Y]
-
     def crossing_to_here(half, from_core):
         return [at(y, half * 2 + takes, flip(z_lo, flip(z0, takes + 1)), from_core) for y in SERVE_Y]
 
@@ -74,7 +71,7 @@
 
     @pl.when(late_0)
     def _():
-        for device in from_early:
+        for device in across(0, 1):
             signal(device)
 
     @pl.when(core == 0)
@@ -170,7 +167,7 @@
 
         @pl.when(early_1)
         def _():
-            for device in to_late:
+            for device in across(1, 0):
                 act(device)
 
         @pl.when(core == 0)

time: 29.5 us -> 28 us (0.949)
  the two profiles are of different devices: /device:TPU:132 before, /device:TPU:1 now
where the time goes in v9:
time: 28 us; the launch traced here: 27.8 us
  Pallas kernels  25.9 us (92%)
  local copies, waits for them, and re-layouts  1.92 us (7%)
    pallas_call x1, Pallas kernels, local(): pl.pallas_call(kernel, out_shape=jax.ShapeDtypeStruct((32, 256), bf16), i...  25.9 us
    unnamed x5, local copies, waits for them, and re-layouts  1.92 us

profile of v9, /device:TPU:1, one launch (start us, length us, event | category | flops | bytes accessed | tf_op | source)
XLA Modules:
  0.0 27.8 jit_solution(11384197343189720846)
XLA Ops:
  0.0 0.0 copy-start
  0.0 0.7 %copy-done = f32[128]{0:T(128)S(1)} copy-done((f32[128]{0:T(128)S(1)}, f32[128]{0:T(128)}, u32[]{:S(2)}) %copy-start) | copy-done | bytes 536
  0.7 0.0 copy-start.1
  0.7 0.7 %copy-done.1 = s32[32]{0:T(128)S(1)} copy-done((s32[32]{0:T(128)S(1)}, s32[32]{0:T(128)}, u32[]{:S(2)}) %copy-start.1) | copy-done | bytes 152
  1.3 25.9 %shard_map.82 = bf16[32,256]{1,0:T(8,128)(2,1)S(1)} custom-call(bf16[32,5120]{1,0:T(8,128)(2,1)} %hidden_hbm.1, bf16[5120,256]{1,0:T(8,128)(2,1)} %base_hbm.1, bf16[64,160]{1,0:T(8,128)(2,1)} %bitcast.10, bf16[16,8,64]{2,1,0:T(8,128)(2,1)} %bitcast.11, f32[1,128]{1,0:T(1,128)S(1)} %bitcast.6, bf16[32,64,128]{2,1,0:T(8,128)(2,1)} %bitcast.8, ...), custom_call_target="tpu_custom_call" | custom-call | flops 260000000 | bytes 4200000 | tf_op jit(solution)/shard_map/pallas_call | solution.py:335
  27.2 0.6 %copy.10 = bf16[32,256]{1,0:T(8,128)(2,1)} copy(bf16[32,256]{1,0:T(8,128)(2,1)S(1)} %shard_map.82) | data formatting | bytes 32768
Async XLA Ops:
  0.0 0.7 %copy-start = (f32[128]{0:T(128)S(1)}, f32[128]{0:T(128)}, u32[]{:S(2)}) copy-start(f32[128]{0:T(128)} %param.12) | copy-start | bytes 1540
  0.7 0.7 %copy-start.1 = (s32[32]{0:T(128)S(1)}, s32[32]{0:T(128)}, u32[]{:S(2)}) copy-start(s32[32]{0:T(128)} %param.15) | copy-start | bytes 388

commit v10 on v9

--- a/solution.py
+++ b/solution.py
@@ -222,15 +222,15 @@
         @pl.when(jnp.logical_or(late_0, early_1))
         def _():
             for group in groups:
-                for s in others[group * 4:group * 4 + 4]:
-                    pass_on(kind, s, group)
+                for k, s in enumerate(others[group * 4:group * 4 + 4]):
+                    pass_on(kind, s, 4 if group == 3 and k > 1 else group)
 
     def from_sibling(kind, group):
         role = core == 1 if group == 0 else jnp.logical_or(early_0, late_1)
 
         @pl.when(role)
         def _():
-            many(kind, (15, 8, 4, 4)[group], send_core, recv_core.at[group]).wait_recv()
+            many(kind, (15, 8, 4, 2, 2)[group], send_core, recv_core.at[group]).wait_recv()
 
     pass_own(up)
     pass_own(down)
@@ -247,6 +247,7 @@
     from_sibling(up, 1)
     from_sibling(up, 2)
     from_sibling(up, 3)
+    from_sibling(up, 4)
 
     lows = ups[...].astype(jnp.float32)
     both = jnp.where(lax.rem(x, 2) == 0, lows[:, :8], lows[:, 8:]).reshape(256, 128)
@@ -280,7 +281,9 @@
     query += project(1 - z1, 1 - takes, (0, 4))
     pass_rest(down, (3,))
     from_sibling(down, 3)
-    query += project(1 - z1, 1 - takes, (4, 8))
+    query += project(1 - z1, 1 - takes, (4, 6))
+    from_sibling(down, 4)
+    query += project(1 - z1, 1 - takes, (6, 8))
 
     gains = gain[...]
     heads = []
@@ -359,7 +362,7 @@
             pltpu.SemaphoreType.DMA((2,)),
             pltpu.SemaphoreType.DMA((2,)),
             pltpu.SemaphoreType.DMA((N_DP, 2)),
-            pltpu.SemaphoreType.DMA((4, 2)),
+            pltpu.SemaphoreType.DMA((5, 2)),
         ],
         compiler_params=pltpu.CompilerParams(
             collective_id=0, has_side_effects=True, vmem_limit_bytes=54 * 2**20 - 100_000

time: 28 us -> 28 us (level)
  no operation moved by 1% of the time
where the time goes in v10:
time: 28 us; the launch traced here: 27.8 us
  Pallas kernels  25.9 us (92%)
  local copies, waits for them, and re-layouts  1.92 us (7%)
    pallas_call x1, Pallas kernels, local(): pl.pallas_call(kernel, out_shape=jax.ShapeDtypeStruct((32, 256), bf16), i...  25.9 us
    unnamed x5, local copies, waits for them, and re-layouts  1.92 us

profile of v10, /device:TPU:1, one launch (start us, length us, event | category | flops | bytes accessed | tf_op | source)
XLA Modules:
  0.0 27.8 jit_solution(4679798277033057017)
XLA Ops:
  0.0 0.0 copy-start
  0.0 0.7 %copy-done = f32[128]{0:T(128)S(1)} copy-done((f32[128]{0:T(128)S(1)}, f32[128]{0:T(128)}, u32[]{:S(2)}) %copy-start) | copy-done | bytes 536
  0.7 0.0 copy-start.1
  0.7 0.7 %copy-done.1 = s32[32]{0:T(128)S(1)} copy-done((s32[32]{0:T(128)S(1)}, s32[32]{0:T(128)}, u32[]{:S(2)}) %copy-start.1) | copy-done | bytes 152
  1.3 25.9 %shard_map.82 = bf16[32,256]{1,0:T(8,128)(2,1)S(1)} custom-call(bf16[32,5120]{1,0:T(8,128)(2,1)} %hidden_hbm.1, bf16[5120,256]{1,0:T(8,128)(2,1)} %base_hbm.1, bf16[64,160]{1,0:T(8,128)(2,1)} %bitcast.10, bf16[16,8,64]{2,1,0:T(8,128)(2,1)} %bitcast.11, f32[1,128]{1,0:T(1,128)S(1)} %bitcast.6, bf16[32,64,128]{2,1,0:T(8,128)(2,1)} %bitcast.8, ...), custom_call_target="tpu_custom_call" | custom-call | flops 260000000 | bytes 4200000 | tf_op jit(solution)/shard_map/pallas_call | solution.py:338
  27.2 0.6 %copy.10 = bf16[32,256]{1,0:T(8,128)(2,1)} copy(bf16[32,256]{1,0:T(8,128)(2,1)S(1)} %shard_map.82) | data formatting | bytes 32768
Async XLA Ops:
  0.0 0.7 %copy-start = (f32[128]{0:T(128)S(1)}, f32[128]{0:T(128)}, u32[]{:S(2)}) copy-start(f32[128]{0:T(128)} %param.12) | copy-start | bytes 1540
  0.7 0.7 %copy-start.1 = (s32[32]{0:T(128)S(1)}, s32[32]{0:T(128)}, u32[]{:S(2)}) copy-start(s32[32]{0:T(128)} %param.15) | copy-start | bytes 388

commit v11 on v9

--- a/solution.py
+++ b/solution.py
@@ -170,14 +170,21 @@
             for device in across(1, 0):
                 act(device)
 
-        @pl.when(core == 0)
-        def _():
-            for device in within(z1):
-                @pl.when(device[0] != dp)
-                def _():
-                    act(device)
+        @pl.when(early_0)
+        def _():
+            serve_within(act)
+
+    def serve_within(act):
+        for device in within(z1):
+            @pl.when(device[0] != dp)
+            def _():
+                act(device)
 
     serve(lambda device: own_up(device).start())
+
+    @pl.when(late_0)
+    def _():
+        serve_within(lambda device: own_up(device).start())
 
     load(0).wait()
     rows = jnp.transpose(lora_in[...].astype(jnp.float32))
@@ -233,6 +240,11 @@
             many(kind, (15, 8, 4, 4)[group], send_core, recv_core.at[group]).wait_recv()
 
     pass_own(up)
+
+    @pl.when(late_0)
+    def _():
+        serve_within(lambda device: own_down(device).start())
+
     pass_own(down)
 
     @pl.when(late)

time: 28 us -> 29.7 us (1.061)
  the two profiles are of different devices: /device:TPU:1 before, /device:TPU:323 now
where the time goes in v11:
time: 29.7 us; the launch traced here: 29.5 us
  Pallas kernels  27.6 us (93%)
  local copies, waits for them, and re-layouts  1.92 us (6%)
    pallas_call x1, Pallas kernels, local(): pl.pallas_call(kernel, out_shape=jax.ShapeDtypeStruct((32, 256), bf16), i...  27.6 us
    unnamed x5, local copies, waits for them, and re-layouts  1.92 us

profile of v11, /device:TPU:323, one launch (start us, length us, event | category | flops | bytes accessed | tf_op | source)
XLA Modules:
  0.0 29.5 jit_solution(12902728776640665735)
XLA Ops:
  0.0 0.0 copy-start
  0.0 0.7 %copy-done = f32[128]{0:T(128)S(1)} copy-done((f32[128]{0:T(128)S(1)}, f32[128]{0:T(128)}, u32[]{:S(2)}) %copy-start) | copy-done | bytes 536
  0.7 0.0 copy-start.1
  0.7 0.7 %copy-done.1 = s32[32]{0:T(128)S(1)} copy-done((s32[32]{0:T(128)S(1)}, s32[32]{0:T(128)}, u32[]{:S(2)}) %copy-start.1) | copy-done | bytes 152
  1.3 27.6 %shard_map.82 = bf16[32,256]{1,0:T(8,128)(2,1)S(1)} custom-call(bf16[32,5120]{1,0:T(8,128)(2,1)} %hidden_hbm.1, bf16[5120,256]{1,0:T(8,128)(2,1)} %base_hbm.1, bf16[64,160]{1,0:T(8,128)(2,1)} %bitcast.10, bf16[16,8,64]{2,1,0:T(8,128)(2,1)} %bitcast.11, f32[1,128]{1,0:T(1,128)S(1)} %bitcast.6, bf16[32,64,128]{2,1,0:T(8,128)(2,1)} %bitcast.8, ...), custom_call_target="tpu_custom_call" | custom-call | flops 260000000 | bytes 4200000 | tf_op jit(solution)/shard_map/pallas_call | solution.py:347
  28.9 0.6 %copy.10 = bf16[32,256]{1,0:T(8,128)(2,1)} copy(bf16[32,256]{1,0:T(8,128)(2,1)S(1)} %shard_map.82) | data formatting | bytes 32768
Async XLA Ops:
  0.0 0.7 %copy-start = (f32[128]{0:T(128)S(1)}, f32[128]{0:T(128)}, u32[]{:S(2)}) copy-start(f32[128]{0:T(128)} %param.12) | copy-start | bytes 1540
  0.7 0.7 %copy-start.1 = (s32[32]{0:T(128)S(1)}, s32[32]{0:T(128)}, u32[]{:S(2)}) copy-start(s32[32]{0:T(128)} %param.15) | copy-start | bytes 388

commit v12 on v9

--- a/solution.py
+++ b/solution.py
@@ -288,14 +288,20 @@
         head = query[:, h * 128:h * 128 + 128]
         inverse = lax.rsqrt(jnp.mean(head * head, axis=-1, keepdims=True) + 1e-06)
         heads.append(head * inverse * gains)
-    parts = []
-    for j in range(4):
-        normed = jnp.concatenate([heads[0][j * 8:j * 8 + 8], heads[1][j * 8:j * 8 + 8]], axis=0).astype(jnp.bfloat16)
-        values_tile = values[j * 8:j * 8 + 8].reshape(512, 128)
-        scores = jnp.dot(normed, turned_keys[j], preferred_element_type=jnp.float32) * (1.0 / math.sqrt(128)) + bias[j]
-        expo = jnp.exp(scores - jnp.max(scores, axis=-1, keepdims=True))
-        weights = (expo * (1.0 / jnp.sum(expo, axis=-1, keepdims=True))).astype(jnp.bfloat16)
-        parts.append(jnp.dot(weights, values_tile, preferred_element_type=jnp.float32))
+    tiles = range(4)
+    normed = [
+        jnp.concatenate([head[j * 8:j * 8 + 8] for head in heads], axis=0).astype(jnp.bfloat16) for j in tiles
+    ]
+    products = [jnp.dot(normed[j], turned_keys[j], preferred_element_type=jnp.float32) for j in tiles]
+    scores = [products[j] * (1.0 / math.sqrt(128)) + bias[j] for j in tiles]
+    highest = [jnp.max(scores[j], axis=-1, keepdims=True) for j in tiles]
+    expo = [jnp.exp(scores[j] - highest[j]) for j in tiles]
+    sums = [jnp.sum(expo[j], axis=-1, keepdims=True) for j in tiles]
+    weights = [(expo[j] * (1.0 / sums[j])).astype(jnp.bfloat16) for j in tiles]
+    parts = [
+        jnp.dot(weights[j], values[j * 8:j * 8 + 8].reshape(512, 128), preferred_element_type=jnp.float32)
+        for j in tiles
+    ]
     out_ref[...] = jnp.concatenate(
         [jnp.concatenate([part[h * 8:h * 8 + 8] for part in parts], axis=0) for h in range(2)], axis=1
     ).astype(jnp.bfloat16)

time: 28 us -> 28 us (level)
  no operation moved by 1% of the time
where the time goes in v12:
time: 28 us; the launch traced here: 27.8 us
  Pallas kernels  25.9 us (92%)
  local copies, waits for them, and re-layouts  1.92 us (7%)
    pallas_call x1, Pallas kernels, local(): pl.pallas_call(kernel, out_shape=jax.ShapeDtypeStruct((32, 256), bf16), i...  25.9 us
    unnamed x5, local copies, waits for them, and re-layouts  1.92 us

profile of v12, /device:TPU:1, one launch (start us, length us, event | category | flops | bytes accessed | tf_op | source)
XLA Modules:
  0.0 27.8 jit_solution(5519766983759097607)
XLA Ops:
  0.0 0.0 copy-start
  0.0 0.7 %copy-done = f32[128]{0:T(128)S(1)} copy-done((f32[128]{0:T(128)S(1)}, f32[128]{0:T(128)}, u32[]{:S(2)}) %copy-start) | copy-done | bytes 536
  0.7 0.0 copy-start.1
  0.7 0.7 %copy-done.1 = s32[32]{0:T(128)S(1)} copy-done((s32[32]{0:T(128)S(1)}, s32[32]{0:T(128)}, u32[]{:S(2)}) %copy-start.1) | copy-done | bytes 152
  1.3 25.9 %shard_map.82 = bf16[32,256]{1,0:T(8,128)(2,1)S(1)} custom-call(bf16[32,5120]{1,0:T(8,128)(2,1)} %hidden_hbm.1, bf16[5120,256]{1,0:T(8,128)(2,1)} %base_hbm.1, bf16[64,160]{1,0:T(8,128)(2,1)} %bitcast.10, bf16[16,8,64]{2,1,0:T(8,128)(2,1)} %bitcast.11, f32[1,128]{1,0:T(1,128)S(1)} %bitcast.6, bf16[32,64,128]{2,1,0:T(8,128)(2,1)} %bitcast.8, ...), custom_call_target="tpu_custom_call" | custom-call | flops 260000000 | bytes 4200000 | tf_op jit(solution)/shard_map/pallas_call | solution.py:341
  27.2 0.6 %copy.10 = bf16[32,256]{1,0:T(8,128)(2,1)} copy(bf16[32,256]{1,0:T(8,128)(2,1)S(1)} %shard_map.82) | data formatting | bytes 32768
Async XLA Ops:
  0.0 0.7 %copy-start = (f32[128]{0:T(128)S(1)}, f32[128]{0:T(128)}, u32[]{:S(2)}) copy-start(f32[128]{0:T(128)} %param.12) | copy-start | bytes 1540
  0.7 0.7 %copy-start.1 = (s32[32]{0:T(128)S(1)}, s32[32]{0:T(128)}, u32[]{:S(2)}) copy-start(s32[32]{0:T(128)} %param.15) | copy-start | bytes 388
